TPU v7x, 128 devices: a whole 4x4x4 slice. The times are simulated.
128 devices in a mesh: rows: 8 (over y, core), cols: 16 (over x, z).
Axes of the slice: x: 4, y: 4, z: 4, core: 2. Of those that a mesh axis runs over, the one named last changes fastest.
Arguments:
- lab_factors: bfloat16 [262144, 256], P(('rows', 'cols')), may hold values from -0.75 to 0.75
- patient_factors: bfloat16 [8192, 256], P('rows'), may hold values from -1.796875 to 1.796875
- values: bfloat16 [8, 1024, 128, 128], P('rows', 'cols'), may hold values from -6 to 6
- weights: bfloat16 [8, 1024, 128, 128], P('rows', 'cols'), may hold values from 0 to 5
- tile_patient: int32 [8, 1024], P('rows', 'cols'), may hold values from 0 to 7, as said below
- tile_lab: int32 [8, 1024], P('rows', 'cols'), may hold values from 0 to 127
- tile_count: int32 [8, 16], P('rows', 'cols'), may hold values from 1 to 64, as said below
- ecg_embed: bfloat16 [8192, 256], P('rows'), may hold values from -6 to 6
- ecg_map: bfloat16 [256, 256], replicated, may hold values from -0.8984375 to 0.8984375
Outputs:
- new_patient: float32 [8192, 256], P(('rows', 'cols'))
- new_lab: float32 [16, 16384, 256], P('cols', 'rows')
Inputs may be any that keep to these rules, and one draw needn't show every extreme that they name: The 64 slots of one device name distinct pairs of tile_patient and tile_lab. The slots of a device from its tile_count on are padding; some device has 64 in every draw.
All inputs are finite; a program needn't handle non-finite values.
Results may differ from a plain program's by a relative error of at most 0.0033.
Values may be sent and summed in bfloat16 or wider, within the bound.
No kernel may reach another device: no remote copies, remote signals or barrier semaphores. Data moves between devices by JAX's collectives and lax.ppermute only.
A program may use at most 128 MiB of HBM per device.

v0:
```python
import functools

import jax
import jax.numpy as jnp
from jax import lax
from jax.experimental import pallas as pl
from jax.experimental.pallas import tpu as pltpu
from jax.sharding import PartitionSpec as P

ITERS = 3
ridge_term = 1.0
highest = lax.Precision.HIGHEST
bf16 = jnp.bfloat16
f32 = jnp.float32
MIB = 1 << 20
BIG = 56

VMEM = pl.BlockSpec(memory_space=pltpu.VMEM)
SMEM = pl.BlockSpec(memory_space=pltpu.SMEM)
ANY = pl.BlockSpec(memory_space=pl.ANY)

GROUP = 8
CHUNK = 6
LAB_CHUNK = 8
SIDE = 4
PASS_TYPES = (f32, bf16)


def dot_nt(a, b):
    return lax.dot_general(a, b, (((1,), (1,)), ((), ())), preferred_element_type=f32)


def dot_nn(a, b):
    return lax.dot_general(a, b, (((1,), (0,)), ((), ())), preferred_element_type=f32)


def prep_kernel(
    tiles, slots, row_ref, patient_ref, lab_ref, count_ref, x_any, w_any, meta_ref, work_ref, xs_any, ws_any, *rest
):
    x_ref, w_ref, tmp, order, fill, x_sem, w_sem, xs_sem, ws_sem = rest[-9:]
    same, other = rest[:-10], rest[-10]
    n = 2 * len(same)
    pieces = [same[k // 2] if k % 2 == 0 else other.at[k // 2] for k in range(n)]
    share = x_any.shape[2] // n
    live = count_ref[0, 0]
    row = row_ref[0]

    def clear(i, carry):
        meta_ref[0, i] = 0
        return carry

    lax.fori_loop(0, meta_ref.shape[1], clear, 0)
    for p in range(tiles + 2):
        fill[p] = 0

    def key_of(s):
        return jnp.where(s < live, patient_ref[0, s], tiles)

    def count(s, carry):
        key = key_of(s)
        fill[key + 1] = fill[key + 1] + 1
        return carry

    lax.fori_loop(0, slots, count, 0)
    for p in range(tiles + 1):
        fill[p + 1] = fill[p + 1] + fill[p]
        meta_ref[0, slots + p] = fill[p]

    def place(s, carry):
        key = key_of(s)
        at = fill[key]
        fill[key] = at + 1
        order[at] = s
        meta_ref[0, at] = lab_ref[0, s]
        return carry

    lax.fori_loop(0, slots, place, 0)

    def at(c):
        return pl.ds(c * GROUP, GROUP)

    def fetch(c, carry):
        for j in range(GROUP):
            s = c * GROUP + j
            pltpu.make_async_copy(x_any.at[order[s]], x_ref.at[s], x_sem.at[c]).start()
            pltpu.make_async_copy(w_any.at[order[s]], w_ref.at[s], w_sem.at[c]).start()
        return carry

    lax.fori_loop(0, slots // GROUP, fetch, 0)

    def hand_on(c):
        return (
            pltpu.make_async_copy(x_ref.at[at(c)], xs_any.at[at(c)], xs_sem.at[c]),
            pltpu.make_async_copy(w_ref.at[at(c)], ws_any.at[at(c)], ws_sem.at[c]),
        )

    def no_work(i, carry):
        for f in range(4):
            work_ref[f, i] = 0
        return carry

    lax.fori_loop(0, work_ref.shape[1], no_work, 0)
    chunks = jnp.int32(0)
    for p in range(tiles):
        lo, hi = meta_ref[0, slots + p], meta_ref[0, slots + p + 1]

        def add(i, carry, p=p, lo=lo, hi=hi, chunks=chunks):
            work_ref[0, chunks + i] = p
            work_ref[1, chunks + i] = lo + i * CHUNK
            work_ref[2, chunks + i] = hi
            return carry

        count_p = (hi - lo + CHUNK - 1) // CHUNK
        lax.fori_loop(0, count_p, add, 0)
        chunks = chunks + count_p

    def pad(i, carry):
        work_ref[2, i] = live
        work_ref[1, i] = live
        return carry

    blocks = (chunks + SIDE - 1) // SIDE
    lax.fori_loop(chunks, blocks * SIDE, pad, 0)
    work_ref[3, 0] = blocks

    lane = lax.broadcasted_iota(jnp.int32, (share, meta_ref.shape[1]), 1)
    table = jnp.zeros(lane.shape, f32)
    for i in range(slots + tiles + 1):
        table = jnp.where(lane == i, meta_ref[0, i].astype(f32), table)
    for k in range(n):
        pieces[k][2 * slots] = table.astype(bf16)

    size = x_any.shape[1]
    eye = (
        lax.broadcasted_iota(jnp.int32, (size, size), 0)
        == lax.broadcasted_iota(jnp.int32, (size, size), 1)
    ).astype(f32).astype(bf16)

    def turn(c, carry):
        pltpu.make_async_copy(x_any.at[at(c)], x_ref.at[at(c)], x_sem.at[c]).wait()
        pltpu.make_async_copy(w_any.at[at(c)], w_ref.at[at(c)], w_sem.at[c]).wait()
        for copy in hand_on(c):
            copy.start()
        for u in range(GROUP):
            tmp[u, 0] = dot_nt(eye, x_ref[c * GROUP + u]).astype(bf16)
            tmp[u, 1] = dot_nt(eye, w_ref[c * GROUP + u]).astype(bf16)
        for u in range(GROUP):
            s = c * GROUP + u
            for k in range(n):
                rows = pl.ds(pl.multiple_of((row ^ k) * share, share), share)
                pieces[k][s] = tmp[u, 0, rows, :]
                pieces[k][slots + s] = tmp[u, 1, rows, :]
        return carry

    lax.fori_loop(0, slots // GROUP, turn, 0)

    def end(c, carry):
        for copy in hand_on(c):
            copy.wait()
        return carry

    lax.fori_loop(0, slots // GROUP, end, 0)


def patient_sums(with_values, work_ref, x_ref, w_ref, v_ref, t_ref, y_ref, out_ref, acc, arrive):
    acc[...] = jnp.zeros_like(acc)

    def chunk(c):
        tile, first, end = [work_ref[f, c] for f in range(3)]
        at = [jnp.maximum(jnp.minimum(first + j, end - 1), 0) for j in range(CHUNK)]
        labs = jnp.concatenate([v_ref[a] for a in at], axis=0)
        turned = jnp.concatenate([t_ref[a] for a in at], axis=1)
        wts = jnp.concatenate(
            [w_ref[a].astype(f32) * (first + j < end).astype(f32) for j, a in enumerate(at)], axis=1
        )
        scores = dot_nn(y_ref[tile], turned)
        if with_values:
            vals = jnp.concatenate([x_ref[a].astype(f32) for a in at], axis=1)
            kern = wts * (vals - scores)
        else:
            kern = wts * scores
        return tile, dot_nn(kern.astype(bf16), labs)

    def block(b, there):
        there = arrive(there, work_ref[2, b * SIDE + SIDE - 1])
        found = [chunk(b * SIDE + j) for j in range(SIDE)]
        for tile, terms in found:
            acc[tile] += terms
        return there

    lax.fori_loop(0, work_ref[3, 0], block, jnp.int32(1))
    out_ref[...] = acc[...].astype(out_ref.dtype)


def first_pass_kernel(
    slots, n, row_ref, meta_ref, work_ref, xs_any, ws_any, y_ref, early_any, here_any, there_any, *refs
):
    out_ref, kept_any, turned_any, v_ref, w_ref, x_ref, acc, v_sem, w_sem, x_sem, kept_sem = refs[:11]
    t_ref, turned_sem = refs[11:]
    row = row_ref[0]
    live = meta_ref[0, slots + y_ref.shape[0]]
    batches = (live + GROUP - 1) // GROUP
    owned = early_any.shape[0] // n
    early = early_any.shape[1]
    late = v_ref.shape[1] - early

    def at(c):
        return pl.ds(c * GROUP, GROUP)

    def rest(c):
        return (
            pltpu.make_async_copy(ws_any.at[at(c)], w_ref.at[at(c)], w_sem.at[c]),
            pltpu.make_async_copy(xs_any.at[at(c)], x_ref.at[at(c)], x_sem.at[c]),
        )

    def keep(c):
        return (
            pltpu.make_async_copy(v_ref.at[at(c)], kept_any.at[at(c)], kept_sem.at[c]),
            pltpu.make_async_copy(t_ref.at[at(c)], turned_any.at[at(c)], turned_sem.at[c]),
        )

    def start(c, carry):
        for j in range(GROUP):
            s = c * GROUP + j
            tile = meta_ref[0, s]
            source = row ^ (tile // owned)
            pltpu.make_async_copy(
                early_any.at[tile], v_ref.at[s, pl.ds(0, early), :], v_sem.at[c]
            ).start()
            for core, late_any in enumerate((here_any, there_any)):

                @pl.when(source % 2 == core)
                def _(late_any=late_any, s=s, tile=tile, source=source):
                    pltpu.make_async_copy(
                        late_any.at[tile % owned, source // 2],
                        v_ref.at[s, pl.ds(early, late), :],
                        v_sem.at[c],
                    ).start()

        for copy in rest(c):
            copy.start()
        return carry

    lax.fori_loop(0, batches, start, 0)

    def wait(c, carry):
        for copy in rest(c):
            copy.wait()
        pltpu.make_async_copy(kept_any.at[at(c)], v_ref.at[at(c)], v_sem.at[c]).wait()
        for j in range(GROUP):
            t_ref[c * GROUP + j] = v_ref[c * GROUP + j].T
        for copy in keep(c):
            copy.start()
        return carry

    wait(0, 0)

    def arrive(there, hi):
        until = jnp.maximum((hi + GROUP - 1) // GROUP, there)
        lax.fori_loop(there, until, wait, 0)
        return until

    patient_sums(True, work_ref, x_ref, w_ref, v_ref, t_ref, y_ref, out_ref, acc, arrive)

    def end(c, carry):
        for copy in keep(c):
            copy.wait()
        return carry

    lax.fori_loop(0, batches, end, 0)


def pass_kernel(
    slots, meta_ref, work_ref, w_ref, kept_any, turned_any, y_ref, out_ref, v_ref, t_ref, acc, v_sem, t_sem
):
    batches = (meta_ref[0, slots + y_ref.shape[0]] + GROUP - 1) // GROUP

    def copies(c):
        at = pl.ds(c * GROUP, GROUP)
        return (
            pltpu.make_async_copy(turned_any.at[at], t_ref.at[at], t_sem.at[c]),
            pltpu.make_async_copy(kept_any.at[at], v_ref.at[at], v_sem.at[c]),
        )

    def start(c, carry):
        for copy in copies(c):
            copy.start()
        return carry

    def wait(c, carry):
        for copy in copies(c):
            copy.wait()
        return carry

    lax.fori_loop(0, batches, start, 0)
    wait(0, 0)

    def arrive(there, hi):
        until = jnp.maximum((hi + GROUP - 1) // GROUP, there)
        lax.fori_loop(there, until, wait, 0)
        return until

    patient_sums(False, work_ref, None, w_ref, v_ref, t_ref, y_ref, out_ref, acc, arrive)


def spread(probe_ref, rows):
    for k in range(probe_ref.shape[0]):
        probe_ref[k] = rows


def first_kernel(recv_ref, start_ref, side_ref, gram_ref, state_ref, probe_ref):
    residual = jnp.sum(recv_ref[...].astype(f32), axis=0) + side_ref[...]
    state_ref[0] = start_ref[...].astype(f32)
    state_ref[1] = residual
    state_ref[2] = residual
    state_ref[3] = (
        jnp.dot(residual, gram_ref[...], precision=highest, preferred_element_type=f32)
        + ridge_term * residual
    )
    spread(probe_ref, residual.astype(bf16))


def step_kernel(turn_ref, recv_ref, state_in, gram_ref, state_ref, probe_ref):
    residual = state_in[1]
    direction = state_in[2]
    applied = jnp.sum(recv_ref[...].astype(f32), axis=0) + state_in[3]
    norm_now = jnp.sum(residual * residual, axis=1, keepdims=True)
    step_size = norm_now / jnp.sum(direction * applied, axis=1, keepdims=True)
    solution_now = state_in[0] + step_size * direction
    state_ref[0] = solution_now
    last = turn_ref[0] == ITERS - 1

    @pl.when(last)
    def _():
        spread(probe_ref, solution_now.astype(bf16))

    @pl.when(jnp.logical_not(last))
    def _():
        residual_next = residual - step_size * applied
        norm_next = jnp.sum(residual_next * residual_next, axis=1, keepdims=True)
        direction_next = residual_next + norm_next / norm_now * direction
        state_ref[1] = residual_next
        state_ref[2] = direction_next
        state_ref[3] = (
            jnp.dot(
                direction_next, gram_ref[...], precision=highest, preferred_element_type=f32
            )
            + ridge_term * direction_next
        )
        spread(probe_ref, direction_next.astype(bf16))


def lab_kernel(slots, n, row_ref, same_any, other_any, *refs):
    pieces = [same_any, other_any.at[0]]
    for ref in refs[: n // 2 - 1]:
        pieces += [ref.at[0], ref.at[1]]
    refs = refs[n // 2 - 1 :]
    f_own, f_two, f_six, f_top, f_low, g_own, g_two, g_six, g_top, g_low = refs[:10]
    early_any, here_any, there_any, out_ref, xw, f_ref, v_ref, acc, probe, curv, p_sem, f_sem, v_sem = refs[10:23]
    coded, table, meta_ref, t_sem, m_sem = refs[23:]
    tiles = f_ref.shape[0] // n
    half = tiles // 2
    share = v_ref.shape[1]
    size = f_ref.shape[1]
    row = row_ref[0]
    t_copies = [
        pltpu.make_async_copy(pieces[k].at[2 * slots], coded.at[k], t_sem.at[k]) for k in range(n)
    ]
    for copy in t_copies:
        copy.start()
    early = early_any.shape[1] // share
    owned = v_ref.shape[0] // n

    @pl.when(row < early)
    def _():
        at = pl.ds(row * share, share)
        pltpu.make_async_copy(early_any.at[:, at, :], v_ref, v_sem).start()

    @pl.when(row >= early)
    def _():
        at = pl.ds((row - early) * share, share)
        for k in range(n):
            part = (here_any, there_any)[k % 2].at[:, k // 2, at, :]
            to = pl.ds((row ^ k) * owned, owned)
            pltpu.make_async_copy(part, v_ref.at[to], v_sem).start()

    factors = {0: [f_own], 1: [g_own], 2: [f_two], 3: [g_two], 6: [f_six], 7: [g_six]}
    factors |= {4: [f_top, f_low], 5: [g_top, g_low]}
    for k in range(n):
        pltpu.make_async_copy(pieces[k], xw.at[k], p_sem.at[k]).start()
        for h, ref in enumerate(factors[k]):
            to = pl.ds((row ^ k) * tiles + h * half, ref.shape[0])
            pltpu.make_async_copy(ref, f_ref.at[to], f_sem.at[k]).start()
    for k, copy in enumerate(t_copies):
        copy.wait()
        table[k : k + 1] = coded[k, 0:1].astype(f32).astype(jnp.int32)
    m_copy = pltpu.make_async_copy(table, meta_ref, m_sem)
    m_copy.start()
    acc[...] = jnp.zeros_like(acc)
    curv[...] = jnp.zeros_like(curv)
    m_copy.wait()
    pltpu.make_async_copy(v_ref, v_ref, v_sem).wait()

    span = LAB_CHUNK * share
    row_slot = lax.broadcasted_iota(jnp.int32, (span, size), 0) // share

    def sweep(terms_of, total, arrive):
        def of_source(k, carry):
            source = row ^ k
            arrive(k, source)
            lo = [meta_ref[k, slots + p] for p in range(tiles)]
            hi = [meta_ref[k, slots + p + 1] for p in range(tiles)]

            def block(i, carry):
                found = []
                for p in range(tiles):
                    first = lo[p] + i * LAB_CHUNK
                    base = jnp.minimum(first, slots - LAB_CHUNK)
                    labs = [meta_ref[k, base + j] for j in range(LAB_CHUNK)]
                    inside = (row_slot >= first - base) & (row_slot < hi[p] - base)
                    wts = xw[k, pl.ds(slots + base, LAB_CHUNK)].reshape(span, size).astype(f32)
                    wts = jnp.where(inside, wts, 0.0)
                    found.append((labs, terms_of(k, base, labs, wts, f_ref[source * tiles + p])))
                for labs, terms in found:
                    for j, t in enumerate(labs):
                        total[t] += terms[j * share : (j + 1) * share]
                return carry

            most = functools.reduce(jnp.maximum, [b - a for a, b in zip(lo, hi)])
            return lax.fori_loop(0, (most + LAB_CHUNK - 1) // LAB_CHUNK, block, carry)

        lax.fori_loop(0, n, of_source, 0)

    def residual_terms(k, base, labs, wts, patients):
        rows = jnp.concatenate([v_ref[t] for t in labs], axis=0)
        vals = xw[k, pl.ds(base, LAB_CHUNK)].reshape(span, size).astype(f32)
        return dot_nn((wts * (vals - dot_nt(rows, patients))).astype(bf16), patients)

    def arrive(k, source):
        pltpu.make_async_copy(xw.at[0], xw.at[k], p_sem.at[k]).wait()
        at = pl.ds(source * tiles, tiles)
        pltpu.make_async_copy(f_ref.at[pl.ds(0, tiles)], f_ref.at[at], f_sem.at[k]).wait()

    sweep(residual_terms, acc, arrive)

    block = 16

    def finish(i, carry):
        at = pl.ds(i * block, block)
        rest = acc[at] - ridge_term * v_ref[at].astype(f32)
        acc[at] = rest
        probe[at] = rest.astype(bf16)
        return carry

    lax.fori_loop(0, acc.shape[0] // block, finish, 0)

    def curvature_terms(k, base, labs, wts, patients):
        rows = jnp.concatenate([probe[t] for t in labs], axis=0)
        inner = dot_nt(rows, patients)
        return wts * inner * inner

    sweep(curvature_terms, curv, lambda k, source: None)

    def emit(i, carry):
        at = pl.ds(i * block, block)
        rest = acc[at]
        norm = jnp.sum(rest * rest, axis=-1, keepdims=True)
        total = jnp.sum(curv[at], axis=-1, keepdims=True) + ridge_term * norm
        out_ref[at] = (norm / total * rest).astype(out_ref.dtype)
        return carry

    lax.fori_loop(0, acc.shape[0] // block, emit, 0)


def shape_of(shape, dtype):
    return jax.ShapeDtypeStruct(shape, dtype)


def params(mib):
    return pltpu.CompilerParams(vmem_limit_bytes=mib * MIB)


def shards(
    lab_factors,
    patient_factors,
    values,
    weights,
    tile_patient,
    tile_lab,
    tile_count,
    ecg_embed,
    ecg_map,
):
    rows = lax.axis_size("rows")
    cols = lax.axis_size("cols")
    size = values.shape[2]
    slots = values.shape[1]
    rank = lab_factors.shape[1]
    owned_tiles = lab_factors.shape[0] // size
    col_tiles = owned_tiles * rows
    patient_rows = patient_factors.shape[0]
    tiles = patient_rows // size
    share_rows = patient_rows // cols
    lab_share = size // rows
    row = lax.axis_index("rows").astype(jnp.int32).reshape(1)
    x, w = values[0], weights[0]

    def swap(array, k):
        return lax.ppermute(array, "rows", [(i, i ^ k) for i in range(rows)])

    def to_columns(array):
        return lax.all_to_all(array, "cols", split_axis=0, concat_axis=0, tiled=True)

    slot_shape = shape_of((slots, size, size), bf16)
    piece = (2 * slots + 1, lab_share, size)
    out_pieces = [shape_of(piece, bf16)] * (rows // 2) + [shape_of((rows // 2, *piece), bf16)]
    prep = pl.pallas_call(
        functools.partial(prep_kernel, tiles, slots),
        out_shape=[shape_of((1, 128), jnp.int32), shape_of((4, 128), jnp.int32)]
        + [slot_shape] * 2
        + out_pieces,
        in_specs=[SMEM] * 4 + [ANY] * 2,
        out_specs=[SMEM] * 2 + [ANY] * 2 + [VMEM] * len(out_pieces),
        scratch_shapes=[
            pltpu.VMEM((slots, size, size), bf16),
            pltpu.VMEM((slots, size, size), bf16),
            pltpu.VMEM((GROUP, 2, size, size), bf16),
            pltpu.SMEM((slots,), jnp.int32),
            pltpu.SMEM((tiles + 2,), jnp.int32),
        ]
        + [pltpu.SemaphoreType.DMA((slots // GROUP,))] * 4,
        compiler_params=params(BIG),
        cost_estimate=pl.CostEstimate(flops=10**9, bytes_accessed=48 * MIB, transcendentals=0),
        name="prep",
    )(row, tile_patient, tile_lab, tile_count, x, w)
    (meta, work, xs, ws), same, other = prep[:4], prep[4:-1], prep[-1]

    early = size - size // 4
    given = lab_factors.reshape(owned_tiles, size, rank)
    late = given[:, early:]
    late = [late] + [swap(late, 2 * h) for h in range(1, rows // 2)]
    own = to_columns(given[:, :early])
    labs = lax.all_gather(own, "rows", axis=0, tiled=True)
    late, _ = lax.optimization_barrier((late, own))
    late_here = to_columns(jnp.stack(late, axis=1))
    late_there = swap(late_here, 1)
    other = swap(other, 1)

    embed_map = ecg_map.astype(f32)
    gram = jnp.dot(embed_map.T, embed_map, precision=highest)
    share_at = lax.axis_index("cols") * share_rows
    start_share = lax.dynamic_slice_in_dim(patient_factors, share_at, share_rows).astype(f32)
    embed_share = lax.dynamic_slice_in_dim(ecg_embed, share_at, share_rows).astype(f32)
    side = (
        jnp.dot(
            embed_share - jnp.dot(start_share, embed_map.T, precision=highest),
            embed_map,
            precision=highest,
        )
        - ridge_term * start_share
    )

    labs, late_here, late_there, same, other = lax.optimization_barrier(
        (labs, late_here, late_there, same, other)
    )
    pieces = [jnp.stack([same[h], other[h]]) for h in range(1, rows // 2)]
    pieces = [swap(piece, 2 * h) for h, piece in enumerate(pieces, 1)]

    def exchange(partial):
        partial = partial.reshape(patient_rows, rank)
        recv = lax.all_to_all(partial, "cols", split_axis=0, concat_axis=0, tiled=True)
        return recv.reshape(cols, share_rows, rank)

    def to_all(probe):
        probe = probe.reshape(patient_rows, rank)
        probe = lax.all_to_all(probe, "cols", split_axis=0, concat_axis=0, tiled=True)
        return probe.reshape(tiles, size, rank)

    state_shape = shape_of((4, share_rows, rank), f32)
    probe_shape = shape_of((cols, share_rows, rank), bf16)
    batches = slots // GROUP
    partial, slot_labs, turned_labs = pl.pallas_call(
        functools.partial(first_pass_kernel, slots, rows),
        out_shape=[
            shape_of((tiles, size, rank), PASS_TYPES[0]),
            shape_of((slots, size, rank), bf16),
            shape_of((slots, rank, size), bf16),
        ],
        in_specs=[SMEM] * 3 + [VMEM] * 3 + [ANY] * 3,
        out_specs=[VMEM, ANY, ANY],
        scratch_shapes=[
            pltpu.VMEM((slots, size, rank), bf16),
            pltpu.VMEM((slots, size, size), bf16),
            pltpu.VMEM((slots, size, size), bf16),
            pltpu.VMEM((tiles, size, rank), f32),
        ]
        + [pltpu.SemaphoreType.DMA((batches,))] * 4
        + [pltpu.VMEM((slots, rank, size), bf16), pltpu.SemaphoreType.DMA((batches,))],
        compiler_params=params(BIG),
        name="first_pass",
    )(
        row,
        meta,
        work,
        xs,
        ws,
        patient_factors.reshape(tiles, size, rank),
        labs,
        late_here,
        late_there,
    )
    state, probe = pl.pallas_call(
        first_kernel,
        out_shape=[state_shape, probe_shape],
        in_specs=[VMEM] * 4,
        out_specs=[VMEM] * 2,
        compiler_params=params(8),
        name="first_step",
    )(exchange(partial), start_share, side, gram)

    def turn(iteration, carry):
        state, probe = carry
        partial = pl.pallas_call(
            functools.partial(pass_kernel, slots),
            out_shape=shape_of((tiles, size, rank), PASS_TYPES[1]),
            in_specs=[SMEM] * 2 + [VMEM, ANY, ANY, VMEM],
            out_specs=VMEM,
            scratch_shapes=[
                pltpu.VMEM((slots, size, rank), bf16),
                pltpu.VMEM((slots, rank, size), bf16),
                pltpu.VMEM((tiles, size, rank), f32),
                pltpu.SemaphoreType.DMA((batches,)),
                pltpu.SemaphoreType.DMA((batches,)),
            ],
            compiler_params=params(28),
            name="patient_pass",
        )(meta, work, ws, slot_labs, turned_labs, to_all(probe))
        state, probe = pl.pallas_call(
            step_kernel,
            out_shape=[state_shape, probe_shape],
            in_specs=[SMEM] + [VMEM] * 3,
            out_specs=[VMEM] * 2,
            compiler_params=params(8),
            name="step",
        )(iteration.reshape(1), exchange(partial), state, gram)
        return state, probe

    state, probe = lax.fori_loop(0, ITERS, turn, (state, probe))
    patient_out = state[0]

    f_own = to_all(probe)
    half = tiles // 2
    f_two, f_six = swap(f_own, 2), swap(f_own, 6)
    f_top, f_low = swap(f_six[:half], 2), swap(f_two[half:], 6)
    here = [f_own, f_two, f_six, f_top, f_low]
    factors = here + [swap(part, 1) for part in here]
    delta = pl.pallas_call(
        functools.partial(lab_kernel, slots, rows),
        out_shape=shape_of((col_tiles, lab_share, rank), bf16),
        in_specs=[SMEM] + [ANY] * (2 + len(pieces) + len(factors) + 3),
        out_specs=VMEM,
        scratch_shapes=[
            pltpu.VMEM((rows, 2 * slots + 1, lab_share, size), bf16),
            pltpu.VMEM((rows * tiles, size, rank), bf16),
            pltpu.VMEM((col_tiles, lab_share, rank), bf16),
            pltpu.VMEM((col_tiles, lab_share, rank), f32),
            pltpu.VMEM((col_tiles, lab_share, rank), bf16),
            pltpu.VMEM((col_tiles, lab_share, size), f32),
            pltpu.SemaphoreType.DMA((rows,)),
            pltpu.SemaphoreType.DMA((rows,)),
            pltpu.SemaphoreType.DMA,
            pltpu.VMEM((rows, lab_share, size), bf16),
            pltpu.VMEM((rows, size), jnp.int32),
            pltpu.SMEM((rows, size), jnp.int32),
            pltpu.SemaphoreType.DMA((rows,)),
            pltpu.SemaphoreType.DMA,
        ],
        compiler_params=params(BIG),
        name="lab_step",
    )(row, same[0], other, *pieces, *factors, labs, late_here, late_there)
    back = lax.all_to_all(
        delta.reshape(col_tiles * lab_share, rank), "rows", split_axis=0, concat_axis=0, tiled=True
    )
    back = back.reshape(rows, owned_tiles, lab_share, rank).transpose(1, 0, 2, 3)
    own_labs = jnp.concatenate([own, late_here[:, 0]], axis=1)
    updated = own_labs.reshape(owned_tiles, rows, lab_share, rank).astype(f32) + back.astype(f32)
    return (patient_out, updated.reshape(1, owned_tiles * size, rank))


def solution(mesh):
    in_specs = (
        P(("rows", "cols"), None),
        P("rows", None),
        P("rows", "cols", None, None),
        P("rows", "cols", None, None),
        P("rows", "cols"),
        P("rows", "cols"),
        P("rows", "cols"),
        P("rows", None),
        P(),
    )
    out_specs = (P(("rows", "cols"), None), P("cols", "rows", None))
    return jax.shard_map(shards, mesh=mesh, in_specs=in_specs, out_specs=out_specs, check_vma=False)
```

profile of v0, /device:TPU:1, one launch (start us, length us, event | category | flops | bytes accessed | tf_op | source)
XLA Modules:
  0.0 299.6 jit_solution(4549874800606501857)
XLA Ops:
  7.2 1.2 slice.36
  8.4 21.7 %all_to_all.58 = bf16[16,96,256]{2,1,0:T(8,128)(2,1)} all-to-all(bf16[16,96,256]{2,1,0:T(8,128)(2,1)S(1)} %slice.36), channel_id=1, replica_groups=mesh['rows'=8,'cols'=16] {'cols'}, dimensions={0} | all-to-all | bytes 1572864 | tf_op jit(solution)/shard_map/all_to_all | solution.py:512
  30.2 1.0 slice.37
  31.1 1.4 collective-permute-start
  32.5 2.6 collective-permute-start.1
  35.8 11.3 %prep.1 = (s32[1,128]{1,0:T(1,128)S(1)}, s32[4,128]{1,0:T(4,128)S(1)}, bf16[64,128,128]{2,1,0:T(8,128)(2,1)}, bf16[64,128,128]{2,1,0:T(8,128)(2,1)S(1)}, bf16[12...) custom-call(s32[1]{0:T(128)} %bitcast.3.row_ref, ...), custom_call_target="tpu_custom_call" | custom-call | flops 1000000000 | bytes 50331648 | tf_op jit(solution)/shard_map/prep/pallas_call | solution.py:517
  47.1 2.6 collective-permute-start.4
  49.7 0.1 pad_maximum_fusion.3
  49.9 15.3 %all_to_all.59.here_any.refs_14_ = bf16[16,4,32,256]{3,2,1,0:T(8,128)(2,1)S(1)} all-to-all(bf16[16,4,32,256]{3,2,1,0:T(8,128)(2,1)S(1)} %pad_maximum_fusion.3), channel_id=1, replica_groups=mesh['rows'=8,'cols'=16] {'cols'}, dimensions={0} | all-to-all | bytes 2097152 | tf_op jit(solution)/shard_map/all_to_all | solution.py:512
  65.1 6.2 %collective-permute-start.3 = (bf16[16,4,32,256]{3,2,1,0:T(8,128)(2,1)S(1)}, bf16[16,4,32,256]{3,2,1,0:T(8,128)(2,1)}, u32[]{:S(2)}, u32[]{:S(2)}) collective-permute-start(bf16[16,4,32,256]{3,2,1,0:T(8,128)(2,1)S(1)} %all_to_all.59.here_any.refs_14_), channel_id=1, source_target_pairs={{0,16},{16,0},{32,48},{48,32},{64,80},{80,64},{96,112},{112,96},{1... | collective-permute-start | bytes 3145736 | tf_op jit(solution)/shard_map/ppermute | solution.py:509
  71.3 0.9 convolution_subtract_fusion.1
  72.2 1.0 fusion.4.gram_ref
  73.2 0.5 collective-permute-done.3.there_any.refs_15_
  73.7 3.8 %all-gather.2.cloned.1.call-done.early_any.refs_13_ = bf16[128,96,256]{2,1,0:T(8,128)(2,1)} async-done(((bf16[16,96,256]{2,1,0:T(8,128)(2,1)}), bf16[128,96,256]{2,1,0:T(8,128)(2,1)}) %all-gather.2.cloned.1.call-update) | async-done | bytes 6291472 | tf_op jit(solution)/shard_map/all_gather | solution.py:543
  77.5 6.3 %first_pass.1 = (f32[8,128,256]{2,1,0:T(8,128)}, bf16[64,128,256]{2,1,0:T(8,128)(2,1)}, bf16[64,256,128]{2,1,0:T(8,128)(2,1)}) custom-call(s32[1]{0:T(128)} %bitcast.3.row_ref, s32[1,128]{1,0:T(1,128)S(1)} %get-tuple-element.285.meta_ref, s32[4,128]{1,0:T(4,128)S(1)} %get-tuple-element.286.work_ref, bf16[64,128,128]{2,1,0:T(8,128)(2,1)} %get-tuple-element.176.xs_any, ...), custom_call_target="tpu_custom_call" | custom-call | tf_op jit(solution)/shard_map/first_pass/pallas_call | solution.py:582
  83.8 4.7 %all-to-all-start.4 = ((f32[16,64,256]{2,1,0:T(8,128)}), f32[16,64,256]{2,1,0:T(8,128)S(1)}, u32[]{:S(2)}, u32[]{:S(2)}) async-start(f32[16,64,256]{2,1,0:T(8,128)} %bitcast.61), calls=%async_computation.4 | async-start | bytes 2097152 | tf_op jit(solution)/shard_map/all_to_all | solution.py:571
  88.5 1.0 convolution_subtract_fusion.side_ref
  89.6 1.7 fusion.3
  91.3 1.1 pad_maximum_fusion
  92.4 1.1 pad_maximum_fusion.1
  93.5 1.1 collective-permute-start.6
  94.6 1.1 pad_maximum_fusion.2
  95.7 2.7 collective-permute-start.7
  98.4 0.8 dynamic-slice_convert_fusion.start_ref
  99.1 4.8 %all-to-all-done.4.recv_ref = f32[16,64,256]{2,1,0:T(8,128)S(1)} async-done(((f32[16,64,256]{2,1,0:T(8,128)}), f32[16,64,256]{2,1,0:T(8,128)S(1)}, u32[]{:S(2)}, u32[]{:S(2)}) %all-to-all-start.4) | async-done | bytes 1048608 | tf_op jit(solution)/shard_map/all_to_all | solution.py:571
  103.9 2.0 first_step.1
  106.0 94.3 %while.15 = (s32[]{:T(128)}, f32[4,64,256]{2,1,0:T(8,128)}, bf16[16,64,256]{2,1,0:T(8,128)(2,1)}, s32[1,128]{1,0:T(1,128)S(1)}, s32[4,128]{1,0:T(4,128)S(1)}, /*...) while((s32[]{:T(128)}, f32[4,64,256]{2,1,0:T(8,128)}, ...), condition=%wide.region_1.0_spmd, body=%wide.region_0.0_spmd.sunk | while | flops 2 | bytes 5243077 | solution.py:648
  106.0 13.0 %all_to_all.61 = bf16[16,64,256]{2,1,0:T(8,128)(2,1)S(1)} all-to-all(bf16[16,64,256]{2,1,0:T(8,128)(2,1)} %get-tuple-element.294), channel_id=1, replica_groups=mesh['rows'=8,'cols'=16] {'cols'}, dimensions={0} | all-to-all | bytes 1048576 | tf_op jit(solution)/shard_map/while/body/eval_jaxpr/all_to_all | solution.py:576
  119.0 4.5 %patient_pass.5 = bf16[8,128,256]{2,1,0:T(8,128)(2,1)} custom-call(s32[1,128]{1,0:T(1,128)S(1)} %get-tuple-element.305.meta_ref, s32[4,128]{1,0:T(4,128)S(1)} %get-tuple-element.306.work_ref, bf16[64,128,128]{2,1,0:T(8,128)(2,1)S(1)} %get-tuple-element.307.w_ref, bf16[64,128,256]{2,1,0:T(8,128)(2,1)} %get-tuple-element.308.kept_any, ...), custom_call_target="tpu_custom_call" | custom-call | tf_op jit(solution)/shard_map/while/body/eval_jaxpr/patient_pass/pallas_call | solution.py:623
  123.5 3.9 %all-to-all-start.1 = ((bf16[16,64,256]{2,1,0:T(8,128)(2,1)}), bf16[16,64,256]{2,1,0:T(8,128)(2,1)S(1)}, u32[]{:S(2)}, u32[]{:S(2)}) async-start(bf16[16,64,256]{2,1,0:T(8,128)(2,1)} %bitcast.47), calls=%async_computation.1 | async-start | bytes 1048576 | tf_op jit(solution)/shard_map/while/body/eval_jaxpr/all_to_all | solution.py:571
  127.5 9.0 %all-to-all-done.1.recv_ref = bf16[16,64,256]{2,1,0:T(8,128)(2,1)S(1)} async-done(((bf16[16,64,256]{2,1,0:T(8,128)(2,1)}), bf16[16,64,256]{2,1,0:T(8,128)(2,1)S(1)}, u32[]{:S(2)}, u32[]{:S(2)}) %all-to-all-start.1) | async-done | bytes 524320 | tf_op jit(solution)/shard_map/while/body/eval_jaxpr/all_to_all | solution.py:571
  136.5 1.5 step.5
  137.9 12.5 %all_to_all.61 = bf16[16,64,256]{2,1,0:T(8,128)(2,1)S(1)} all-to-all(bf16[16,64,256]{2,1,0:T(8,128)(2,1)} %get-tuple-element.294), channel_id=1, replica_groups=mesh['rows'=8,'cols'=16] {'cols'}, dimensions={0} | all-to-all | bytes 1048576 | tf_op jit(solution)/shard_map/while/body/eval_jaxpr/all_to_all | solution.py:576
  150.4 4.5 %patient_pass.5 = bf16[8,128,256]{2,1,0:T(8,128)(2,1)} custom-call(s32[1,128]{1,0:T(1,128)S(1)} %get-tuple-element.305.meta_ref, s32[4,128]{1,0:T(4,128)S(1)} %get-tuple-element.306.work_ref, bf16[64,128,128]{2,1,0:T(8,128)(2,1)S(1)} %get-tuple-element.307.w_ref, bf16[64,128,256]{2,1,0:T(8,128)(2,1)} %get-tuple-element.308.kept_any, ...), custom_call_target="tpu_custom_call" | custom-call | tf_op jit(solution)/shard_map/while/body/eval_jaxpr/patient_pass/pallas_call | solution.py:623
  155.0 3.9 %all-to-all-start.1 = ((bf16[16,64,256]{2,1,0:T(8,128)(2,1)}), bf16[16,64,256]{2,1,0:T(8,128)(2,1)S(1)}, u32[]{:S(2)}, u32[]{:S(2)}) async-start(bf16[16,64,256]{2,1,0:T(8,128)(2,1)} %bitcast.47), calls=%async_computation.1 | async-start | bytes 1048576 | tf_op jit(solution)/shard_map/while/body/eval_jaxpr/all_to_all | solution.py:571
  158.9 8.9 %all-to-all-done.1.recv_ref = bf16[16,64,256]{2,1,0:T(8,128)(2,1)S(1)} async-done(((bf16[16,64,256]{2,1,0:T(8,128)(2,1)}), bf16[16,64,256]{2,1,0:T(8,128)(2,1)S(1)}, u32[]{:S(2)}, u32[]{:S(2)}) %all-to-all-start.1) | async-done | bytes 524320 | tf_op jit(solution)/shard_map/while/body/eval_jaxpr/all_to_all | solution.py:571
  167.8 1.5 step.5
  169.3 12.5 %all_to_all.61 = bf16[16,64,256]{2,1,0:T(8,128)(2,1)S(1)} all-to-all(bf16[16,64,256]{2,1,0:T(8,128)(2,1)} %get-tuple-element.294), channel_id=1, replica_groups=mesh['rows'=8,'cols'=16] {'cols'}, dimensions={0} | all-to-all | bytes 1048576 | tf_op jit(solution)/shard_map/while/body/eval_jaxpr/all_to_all | solution.py:576
  181.7 4.5 %patient_pass.5 = bf16[8,128,256]{2,1,0:T(8,128)(2,1)} custom-call(s32[1,128]{1,0:T(1,128)S(1)} %get-tuple-element.305.meta_ref, s32[4,128]{1,0:T(4,128)S(1)} %get-tuple-element.306.work_ref, bf16[64,128,128]{2,1,0:T(8,128)(2,1)S(1)} %get-tuple-element.307.w_ref, bf16[64,128,256]{2,1,0:T(8,128)(2,1)} %get-tuple-element.308.kept_any, ...), custom_call_target="tpu_custom_call" | custom-call | tf_op jit(solution)/shard_map/while/body/eval_jaxpr/patient_pass/pallas_call | solution.py:623
  186.3 3.9 %all-to-all-start.1 = ((bf16[16,64,256]{2,1,0:T(8,128)(2,1)}), bf16[16,64,256]{2,1,0:T(8,128)(2,1)S(1)}, u32[]{:S(2)}, u32[]{:S(2)}) async-start(bf16[16,64,256]{2,1,0:T(8,128)(2,1)} %bitcast.47), calls=%async_computation.1 | async-start | bytes 1048576 | tf_op jit(solution)/shard_map/while/body/eval_jaxpr/all_to_all | solution.py:571
  190.2 8.9 %all-to-all-done.1.recv_ref = bf16[16,64,256]{2,1,0:T(8,128)(2,1)S(1)} async-done(((bf16[16,64,256]{2,1,0:T(8,128)(2,1)}), bf16[16,64,256]{2,1,0:T(8,128)(2,1)S(1)}, u32[]{:S(2)}, u32[]{:S(2)}) %all-to-all-start.1) | async-done | bytes 524320 | tf_op jit(solution)/shard_map/while/body/eval_jaxpr/all_to_all | solution.py:571
  199.1 1.2 step.5
  200.3 13.1 %all_to_all.60 = bf16[16,64,256]{2,1,0:T(8,128)(2,1)S(1)} all-to-all(bf16[16,64,256]{2,1,0:T(8,128)(2,1)} %get-tuple-element.201), channel_id=1, replica_groups=mesh['rows'=8,'cols'=16] {'cols'}, dimensions={0} | all-to-all | bytes 1048576 | tf_op jit(solution)/shard_map/all_to_all | solution.py:576
  213.4 1.3 collective-permute-start.9
  214.7 12.2 %collective-permute-start.8 = (bf16[8,128,256]{2,1,0:T(8,128)(2,1)S(1)}, bf16[8,128,256]{2,1,0:T(8,128)(2,1)S(1)}, u32[]{:S(2)}, u32[]{:S(2)}) collective-permute-start(bf16[8,128,256]{2,1,0:T(8,128)(2,1)S(1)} %bitcast.53), channel_id=1, source_target_pairs={{0,32},{16,48},{32,0},{48,16},{64,96},{80,112},{96,64},{112,80},{1... | collective-permute-start | bytes 1572872 | tf_op jit(solution)/shard_map/ppermute | solution.py:509
  226.9 10.1 %collective-permute-start.12 = (bf16[8,128,256]{2,1,0:T(8,128)(2,1)S(1)}, bf16[8,128,256]{2,1,0:T(8,128)(2,1)S(1)}, u32[]{:S(2)}, u32[]{:S(2)}) collective-permute-start(bf16[8,128,256]{2,1,0:T(8,128)(2,1)S(1)} %bitcast.54), channel_id=1, source_target_pairs={{0,16},{16,0},{32,48},{48,32},{64,80},{80,64},{96,112},{112,96},{1... | collective-permute-start | bytes 1572872 | tf_op jit(solution)/shard_map/ppermute | solution.py:509
  237.0 4.4 %collective-permute-start.10 = (bf16[4,128,256]{2,1,0:T(8,128)(2,1)S(1)}, bf16[4,128,256]{2,1,0:T(8,128)(2,1)S(1)}, u32[]{:S(2)}, u32[]{:S(2)}) collective-permute-start(bf16[4,128,256]{2,1,0:T(8,128)(2,1)S(1)} %slice.38), channel_id=1, source_target_pairs={{0,32},{16,48},{32,0},{48,16},{64,96},{80,112},{96,64},{112,80},{1... | collective-permute-start | bytes 786440 | tf_op jit(solution)/shard_map/ppermute | solution.py:509
  241.4 0.4 collective-permute-start.13
  241.7 0.2 collective-permute-start.14
  242.0 1.8 collective-permute-start.11
  243.8 4.1 %collective-permute-done.10.refs_6_ = bf16[4,128,256]{2,1,0:T(8,128)(2,1)S(1)} collective-permute-done((bf16[4,128,256]{2,1,0:T(8,128)(2,1)S(1)}, bf16[4,128,256]{2,1,0:T(8,128)(2,1)S(1)}, u32[]{:S(2)}, u32[]{:S(2)}) %collective-permute-start.10) | collective-permute-done | bytes 262176 | tf_op jit(solution)/shard_map/ppermute | solution.py:509
  247.9 0.7 collective-permute-start.15
  248.6 2.2 collective-permute-done.11.refs_7_
  250.8 1.1 collective-permute-start.16
  252.0 1.1 collective-permute-done.16.refs_12_
  253.1 0.7 copy-done.17
  253.8 16.7 %lab_step.1 = bf16[128,16,256]{2,1,0:T(8,128)(2,1)} custom-call(s32[1]{0:T(128)} %bitcast.3.row_ref, bf16[129,16,128]{2,1,0:T(8,128)(2,1)} %get-tuple-element.196.same_any, bf16[4,129,16,128]{3,2,1,0:T(8,128)(2,1)} %collective-permute-done.4.other_any, bf16[2,129,16,128]{3,2,1,0:T(8,128)(2,1)} %collective-permute-done.5.refs_0_, ...), custom_call_target="tpu_custom_call" | custom-call | tf_op jit(solution)/shard_map/lab_step/pallas_call | solution.py:657
  270.6 4.0 %all-to-all-start.6 = ((bf16[8,256,256]{2,1,0:T(8,128)(2,1)}), bf16[8,256,256]{2,1,0:T(8,128)(2,1)S(1)}, u32[]{:S(2)}, u32[]{:S(2)}) async-start(bf16[8,256,256]{2,1,0:T(8,128)(2,1)} %bitcast.49), calls=%async_computation.6 | async-start | bytes 2097152 | tf_op jit(solution)/shard_map/all_to_all | solution.py:681
  274.5 1.0 slice_bitcast_fusion
  275.5 1.1 pad_maximum_fusion.4
  276.6 1.5 slice_bitcast_fusion.1
  278.1 11.6 %all-to-all-done.6 = bf16[8,256,256]{2,1,0:T(8,128)(2,1)S(1)} async-done(((bf16[8,256,256]{2,1,0:T(8,128)(2,1)}), bf16[8,256,256]{2,1,0:T(8,128)(2,1)S(1)}, u32[]{:S(2)}, u32[]{:S(2)}) %all-to-all-start.6) | async-done | bytes 1048608 | tf_op jit(solution)/shard_map/all_to_all | solution.py:681
  289.7 1.6 fusion
  291.2 1.6 copy.27
  (65 shorter events, 0.3 us)
Async XLA Ops:
  7.2 64.1 %copy-start = (bf16[256,256]{1,0:T(8,128)(2,1)S(1)}, bf16[256,256]{1,0:T(8,128)(2,1)}, u32[]{:S(2)}) copy-start(bf16[256,256]{1,0:T(8,128)(2,1)} %param.19) | copy-start | bytes 393220
  7.2 70.3 %all-gather.2.cloned.1.call-start = ((), (), s32[]{:S(2)}) async-start(), calls=%async_computation.7 | async-start | bytes 7077888 | tf_op jit(solution)/shard_map/all_gather | solution.py:543
  31.1 18.6 %collective-permute-start = (bf16[16,32,256]{2,1,0:T(8,128)(2,1)S(1)}, bf16[16,32,256]{2,1,0:T(8,128)(2,1)S(1)}, u32[]{:S(2)}, u32[]{:S(2)}) collective-permute-start(bf16[16,32,256]{2,1,0:T(8,128)(2,1)S(1)} %slice.37), channel_id=1, source_target_pairs={{0,32},{16,48},{32,0},{48,16},{64,96},{80,112},{96,64},{112,80},{1... | collective-permute-start | bytes 786440 | tf_op jit(solution)/shard_map/ppermute | solution.py:509
  32.5 17.2 %collective-permute-start.1 = (bf16[16,32,256]{2,1,0:T(8,128)(2,1)S(1)}, bf16[16,32,256]{2,1,0:T(8,128)(2,1)S(1)}, u32[]{:S(2)}, u32[]{:S(2)}) collective-permute-start(bf16[16,32,256]{2,1,0:T(8,128)(2,1)S(1)} %slice.37), channel_id=1, source_target_pairs={{0,64},{16,80},{32,96},{48,112},{64,0},{80,16},{96,32},{112,48},{1... | collective-permute-start | bytes 786440 | tf_op jit(solution)/shard_map/ppermute | solution.py:509
  35.1 14.6 %collective-permute-start.2 = (bf16[16,32,256]{2,1,0:T(8,128)(2,1)S(1)}, bf16[16,32,256]{2,1,0:T(8,128)(2,1)S(1)}, u32[]{:S(2)}, u32[]{:S(2)}) collective-permute-start(bf16[16,32,256]{2,1,0:T(8,128)(2,1)S(1)} %slice.37), channel_id=1, source_target_pairs={{0,96},{16,112},{32,64},{48,80},{64,32},{80,48},{96,0},{112,16},{1... | collective-permute-start | bytes 786440 | tf_op jit(solution)/shard_map/ppermute | solution.py:509
  47.1 26.1 %collective-permute-start.4 = (bf16[4,129,16,128]{3,2,1,0:T(8,128)(2,1)}, bf16[4,129,16,128]{3,2,1,0:T(8,128)(2,1)}, u32[]{:S(2)}, u32[]{:S(2)}) collective-permute-start(bf16[4,129,16,128]{3,2,1,0:T(8,128)(2,1)} %get-tuple-element.186), channel_id=1, source_target_pairs={{0,16},{16,0},{32,48},{48,32},{64,80},{80,64},{96,112},{112,96},{1... | collective-permute-start | bytes 6340616 | tf_op jit(solution)/shard_map/ppermute | solution.py:509
  65.1 12.3 %copy-start.2 = (bf16[16,4,32,256]{3,2,1,0:T(8,128)(2,1)}, bf16[16,4,32,256]{3,2,1,0:T(8,128)(2,1)S(1)}, u32[]{:S(2)}) copy-start(bf16[16,4,32,256]{3,2,1,0:T(8,128)(2,1)S(1)} %all_to_all.59.here_any.refs_14_) | copy-start | bytes 3145732
  65.1 8.6 %collective-permute-start.3 = (bf16[16,4,32,256]{3,2,1,0:T(8,128)(2,1)S(1)}, bf16[16,4,32,256]{3,2,1,0:T(8,128)(2,1)}, u32[]{:S(2)}, u32[]{:S(2)}) collective-permute-start(bf16[16,4,32,256]{3,2,1,0:T(8,128)(2,1)S(1)} %all_to_all.59.here_any.refs_14_), channel_id=1, source_target_pairs={{0,16},{16,0},{32,48},{48,32},{64,80},{80,64},{96,112},{112,96},{1... | collective-permute-start | bytes 3145736 | tf_op jit(solution)/shard_map/ppermute | solution.py:509
  83.8 20.1 %all-to-all-start.4 = ((f32[16,64,256]{2,1,0:T(8,128)}), f32[16,64,256]{2,1,0:T(8,128)S(1)}, u32[]{:S(2)}, u32[]{:S(2)}) async-start(f32[16,64,256]{2,1,0:T(8,128)} %bitcast.61), calls=%async_computation.4 | async-start | bytes 2097152 | tf_op jit(solution)/shard_map/all_to_all | solution.py:571
  88.5 2.8 copy-start.10
  89.6 2.8 copy-start.9
  91.3 3.3 %copy-start.8 = (bf16[129,16,128]{2,1,0:T(8,128)(2,1)S(1)}, bf16[129,16,128]{2,1,0:T(8,128)(2,1)}, u32[]{:S(2)}) copy-start(bf16[129,16,128]{2,1,0:T(8,128)(2,1)} %get-tuple-element.200) | copy-start | bytes 1585156
  92.4 149.0 %collective-permute-start.5 = (bf16[2,129,16,128]{3,2,1,0:T(8,128)(2,1)}, bf16[2,129,16,128]{3,2,1,0:T(8,128)(2,1)}, u32[]{:S(2)}, u32[]{:S(2)}) collective-permute-start(bf16[2,129,16,128]{3,2,1,0:T(8,128)(2,1)} %pad_maximum_fusion), channel_id=1, source_target_pairs={{0,32},{16,48},{32,0},{48,16},{64,96},{80,112},{96,64},{112,80},{1... | collective-permute-start | bytes 3170312 | tf_op jit(solution)/shard_map/ppermute | solution.py:509
  93.5 148.3 %collective-permute-start.6 = (bf16[2,129,16,128]{3,2,1,0:T(8,128)(2,1)}, bf16[2,129,16,128]{3,2,1,0:T(8,128)(2,1)}, u32[]{:S(2)}, u32[]{:S(2)}) collective-permute-start(bf16[2,129,16,128]{3,2,1,0:T(8,128)(2,1)} %pad_maximum_fusion.1), channel_id=1, source_target_pairs={{0,64},{16,80},{32,96},{48,112},{64,0},{80,16},{96,32},{112,48},{1... | collective-permute-start | bytes 3170312 | tf_op jit(solution)/shard_map/ppermute | solution.py:509
  95.7 146.3 %collective-permute-start.7 = (bf16[2,129,16,128]{3,2,1,0:T(8,128)(2,1)}, bf16[2,129,16,128]{3,2,1,0:T(8,128)(2,1)}, u32[]{:S(2)}, u32[]{:S(2)}) collective-permute-start(bf16[2,129,16,128]{3,2,1,0:T(8,128)(2,1)} %pad_maximum_fusion.2), channel_id=1, source_target_pairs={{0,96},{16,112},{32,64},{48,80},{64,32},{80,48},{96,0},{112,16},{1... | collective-permute-start | bytes 3170312 | tf_op jit(solution)/shard_map/ppermute | solution.py:509
  119.0 8.4 %copy-start.3 = (f32[4,64,256]{2,1,0:T(8,128)S(1)}, f32[4,64,256]{2,1,0:T(8,128)}, u32[]{:S(2)}) copy-start(f32[4,64,256]{2,1,0:T(8,128)} %get-tuple-element.293) | copy-start | bytes 786436 | tf_op jit(solution)/shard_map/while
  119.0 17.5 %copy-start.1 = (f32[256,256]{1,0:T(8,128)S(1)}, f32[256,256]{1,0:T(8,128)}, u32[]{:S(2)}) copy-start(f32[256,256]{1,0:T(8,128)} %get-tuple-element.310.gram_ref) | copy-start | bytes 786436 | tf_op jit(solution)/shard_map/while
  123.5 12.9 %all-to-all-start.1 = ((bf16[16,64,256]{2,1,0:T(8,128)(2,1)}), bf16[16,64,256]{2,1,0:T(8,128)(2,1)S(1)}, u32[]{:S(2)}, u32[]{:S(2)}) async-start(bf16[16,64,256]{2,1,0:T(8,128)(2,1)} %bitcast.47), calls=%async_computation.1 | async-start | bytes 1048576 | tf_op jit(solution)/shard_map/while/body/eval_jaxpr/all_to_all | solution.py:571
  150.4 8.4 %copy-start.3 = (f32[4,64,256]{2,1,0:T(8,128)S(1)}, f32[4,64,256]{2,1,0:T(8,128)}, u32[]{:S(2)}) copy-start(f32[4,64,256]{2,1,0:T(8,128)} %get-tuple-element.293) | copy-start | bytes 786436 | tf_op jit(solution)/shard_map/while
  150.4 17.4 %copy-start.1 = (f32[256,256]{1,0:T(8,128)S(1)}, f32[256,256]{1,0:T(8,128)}, u32[]{:S(2)}) copy-start(f32[256,256]{1,0:T(8,128)} %get-tuple-element.310.gram_ref) | copy-start | bytes 786436 | tf_op jit(solution)/shard_map/while
  155.0 12.8 %all-to-all-start.1 = ((bf16[16,64,256]{2,1,0:T(8,128)(2,1)}), bf16[16,64,256]{2,1,0:T(8,128)(2,1)S(1)}, u32[]{:S(2)}, u32[]{:S(2)}) async-start(bf16[16,64,256]{2,1,0:T(8,128)(2,1)} %bitcast.47), calls=%async_computation.1 | async-start | bytes 1048576 | tf_op jit(solution)/shard_map/while/body/eval_jaxpr/all_to_all | solution.py:571
  181.7 8.4 %copy-start.3 = (f32[4,64,256]{2,1,0:T(8,128)S(1)}, f32[4,64,256]{2,1,0:T(8,128)}, u32[]{:S(2)}) copy-start(f32[4,64,256]{2,1,0:T(8,128)} %get-tuple-element.293) | copy-start | bytes 786436 | tf_op jit(solution)/shard_map/while
  181.7 17.4 %copy-start.1 = (f32[256,256]{1,0:T(8,128)S(1)}, f32[256,256]{1,0:T(8,128)}, u32[]{:S(2)}) copy-start(f32[256,256]{1,0:T(8,128)} %get-tuple-element.310.gram_ref) | copy-start | bytes 786436 | tf_op jit(solution)/shard_map/while
  186.3 12.8 %all-to-all-start.1 = ((bf16[16,64,256]{2,1,0:T(8,128)(2,1)}), bf16[16,64,256]{2,1,0:T(8,128)(2,1)S(1)}, u32[]{:S(2)}, u32[]{:S(2)}) async-start(bf16[16,64,256]{2,1,0:T(8,128)(2,1)} %bitcast.47), calls=%async_computation.1 | async-start | bytes 1048576 | tf_op jit(solution)/shard_map/while/body/eval_jaxpr/all_to_all | solution.py:571
  213.4 39.7 %copy-start.5 = (bf16[16,64,256]{2,1,0:T(8,128)(2,1)}, bf16[16,64,256]{2,1,0:T(8,128)(2,1)S(1)}, u32[]{:S(2)}) copy-start(bf16[16,64,256]{2,1,0:T(8,128)(2,1)S(1)} %all_to_all.60) | copy-start | bytes 1572868
  213.4 13.5 %collective-permute-start.9 = (bf16[8,128,256]{2,1,0:T(8,128)(2,1)S(1)}, bf16[8,128,256]{2,1,0:T(8,128)(2,1)S(1)}, u32[]{:S(2)}, u32[]{:S(2)}) collective-permute-start(bf16[8,128,256]{2,1,0:T(8,128)(2,1)S(1)} %bitcast.52), channel_id=1, source_target_pairs={{0,96},{16,112},{32,64},{48,80},{64,32},{80,48},{96,0},{112,16},{1... | collective-permute-start | bytes 1572872 | tf_op jit(solution)/shard_map/ppermute | solution.py:509
  214.7 22.3 %collective-permute-start.8 = (bf16[8,128,256]{2,1,0:T(8,128)(2,1)S(1)}, bf16[8,128,256]{2,1,0:T(8,128)(2,1)S(1)}, u32[]{:S(2)}, u32[]{:S(2)}) collective-permute-start(bf16[8,128,256]{2,1,0:T(8,128)(2,1)S(1)} %bitcast.53), channel_id=1, source_target_pairs={{0,32},{16,48},{32,0},{48,16},{64,96},{80,112},{96,64},{112,80},{1... | collective-permute-start | bytes 1572872 | tf_op jit(solution)/shard_map/ppermute | solution.py:509
  226.9 26.2 %copy-start.6 = (bf16[8,128,256]{2,1,0:T(8,128)(2,1)}, bf16[8,128,256]{2,1,0:T(8,128)(2,1)S(1)}, u32[]{:S(2)}) copy-start(bf16[8,128,256]{2,1,0:T(8,128)(2,1)S(1)} %collective-permute-done.9.refs_5_) | copy-start | bytes 1572868
  226.9 25.0 %collective-permute-start.12 = (bf16[8,128,256]{2,1,0:T(8,128)(2,1)S(1)}, bf16[8,128,256]{2,1,0:T(8,128)(2,1)S(1)}, u32[]{:S(2)}, u32[]{:S(2)}) collective-permute-start(bf16[8,128,256]{2,1,0:T(8,128)(2,1)S(1)} %bitcast.54), channel_id=1, source_target_pairs={{0,16},{16,0},{32,48},{48,32},{64,80},{80,64},{96,112},{112,96},{1... | collective-permute-start | bytes 1572872 | tf_op jit(solution)/shard_map/ppermute | solution.py:509
  237.0 16.1 %copy-start.7 = (bf16[8,128,256]{2,1,0:T(8,128)(2,1)}, bf16[8,128,256]{2,1,0:T(8,128)(2,1)S(1)}, u32[]{:S(2)}) copy-start(bf16[8,128,256]{2,1,0:T(8,128)(2,1)S(1)} %collective-permute-done.8.refs_4_) | copy-start | bytes 1572868
  237.0 10.9 %collective-permute-start.10 = (bf16[4,128,256]{2,1,0:T(8,128)(2,1)S(1)}, bf16[4,128,256]{2,1,0:T(8,128)(2,1)S(1)}, u32[]{:S(2)}, u32[]{:S(2)}) collective-permute-start(bf16[4,128,256]{2,1,0:T(8,128)(2,1)S(1)} %slice.38), channel_id=1, source_target_pairs={{0,32},{16,48},{32,0},{48,16},{64,96},{80,112},{96,64},{112,80},{1... | collective-permute-start | bytes 786440 | tf_op jit(solution)/shard_map/ppermute | solution.py:509
  241.4 10.5 %collective-permute-start.13 = (bf16[8,128,256]{2,1,0:T(8,128)(2,1)S(1)}, bf16[8,128,256]{2,1,0:T(8,128)(2,1)S(1)}, u32[]{:S(2)}, u32[]{:S(2)}) collective-permute-start(bf16[8,128,256]{2,1,0:T(8,128)(2,1)S(1)} %collective-permute-done.8.refs_4_), channel_id=1, source_target_pairs={{0,16},{16,0},{32,48},{48,32},{64,80},{80,64},{96,112},{112,96},{1... | collective-permute-start | bytes 1572872 | tf_op jit(solution)/shard_map/ppermute | solution.py:509
  241.7 10.2 %collective-permute-start.14 = (bf16[8,128,256]{2,1,0:T(8,128)(2,1)S(1)}, bf16[8,128,256]{2,1,0:T(8,128)(2,1)S(1)}, u32[]{:S(2)}, u32[]{:S(2)}) collective-permute-start(bf16[8,128,256]{2,1,0:T(8,128)(2,1)S(1)} %collective-permute-done.9.refs_5_), channel_id=1, source_target_pairs={{0,16},{16,0},{32,48},{48,32},{64,80},{80,64},{96,112},{112,96},{1... | collective-permute-start | bytes 1572872 | tf_op jit(solution)/shard_map/ppermute | solution.py:509
  242.0 8.8 %collective-permute-start.11 = (bf16[4,128,256]{2,1,0:T(8,128)(2,1)S(1)}, bf16[4,128,256]{2,1,0:T(8,128)(2,1)S(1)}, u32[]{:S(2)}, u32[]{:S(2)}) collective-permute-start(bf16[4,128,256]{2,1,0:T(8,128)(2,1)S(1)} %slice.39), channel_id=1, source_target_pairs={{0,96},{16,112},{32,64},{48,80},{64,32},{80,48},{96,0},{112,16},{1... | collective-permute-start | bytes 786440 | tf_op jit(solution)/shard_map/ppermute | solution.py:509
  247.9 5.2 %copy-start.14 = (bf16[4,128,256]{2,1,0:T(8,128)(2,1)}, bf16[4,128,256]{2,1,0:T(8,128)(2,1)S(1)}, u32[]{:S(2)}) copy-start(bf16[4,128,256]{2,1,0:T(8,128)(2,1)S(1)} %collective-permute-done.10.refs_6_) | copy-start | bytes 786436
  247.9 4.1 %collective-permute-start.15 = (bf16[4,128,256]{2,1,0:T(8,128)(2,1)S(1)}, bf16[4,128,256]{2,1,0:T(8,128)(2,1)S(1)}, u32[]{:S(2)}, u32[]{:S(2)}) collective-permute-start(bf16[4,128,256]{2,1,0:T(8,128)(2,1)S(1)} %collective-permute-done.10.refs_6_), channel_id=1, source_target_pairs={{0,16},{16,0},{32,48},{48,32},{64,80},{80,64},{96,112},{112,96},{1... | collective-permute-start | bytes 786440 | tf_op jit(solution)/shard_map/ppermute | solution.py:509
  250.8 2.3 copy-start.15
  250.8 2.3 collective-permute-start.16
  251.9 1.2 copy-start.11
  251.9 1.2 copy-start.12
  251.9 1.2 copy-start.13
  251.9 1.2 copy-start.16
  253.1 0.7 copy-start.17
  270.5 5.0 %copy-start.4 = (bf16[16,96,256]{2,1,0:T(8,128)(2,1)S(1)}, bf16[16,96,256]{2,1,0:T(8,128)(2,1)}, u32[]{:S(2)}) copy-start(bf16[16,96,256]{2,1,0:T(8,128)(2,1)} %all_to_all.58) | copy-start | bytes 2359300
  270.6 19.1 %all-to-all-start.6 = ((bf16[8,256,256]{2,1,0:T(8,128)(2,1)}), bf16[8,256,256]{2,1,0:T(8,128)(2,1)S(1)}, u32[]{:S(2)}, u32[]{:S(2)}) async-start(bf16[8,256,256]{2,1,0:T(8,128)(2,1)} %bitcast.49), calls=%async_computation.6 | async-start | bytes 2097152 | tf_op jit(solution)/shard_map/all_to_all | solution.py:681
Sparse Core Ops, SparseCore 0:
  30.3 47.1 all-gather.1
where the time goes:
time: 299 us; the launch traced here: 300 us
  blocking collectives  88 us (29%)
  starting transfers between devices  69.1 us (23%)
  waiting for transfers between devices  54.9 us (18%)
  Pallas kernels  54.1 us (18%)
  between operations  15 us (5%)
  local copies, waits for them, and re-layouts  8.76 us (3%)
  other arithmetic  6.74 us (2%)
    all_to_all x4, blocking collectives, to_all(): lax.all_to_all(probe, 'cols', split_axis=0, concat_axis=0, tiled=True)  51.1 us
    ppermute x17, starting transfers between devices, swap(): return lax.ppermute(array, 'rows', [(i, i ^ k) for i in range(rows)])  48.7 us
    all_to_all x2, blocking collectives, to_columns(): lax.all_to_all(array, 'cols', split_axis=0, concat_axis=0, tiled=True)  37 us
    all_to_all x4, waiting for transfers between devices, exchange(): lax.all_to_all(partial, 'cols', split_axis=0, concat_axis=0, tiled=True)  31.6 us
    pallas_call x1, Pallas kernels, shards(): pl.pallas_call(functools.partial(lab_kernel, slots, rows), out_shape=shap...  16.7 us
    all_to_all x4, starting transfers between devices, exchange(): lax.all_to_all(partial, 'cols', split_axis=0, concat_axis=0, tiled=True)  16.4 us
    pallas_call x3, Pallas kernels, turn(): pl.pallas_call(functools.partial(pass_kernel, slots), out_shape=shape_of(...  13.6 us
    all_to_all x1, waiting for transfers between devices, shards(): lax.all_to_all(delta.reshape(col_tiles * lab_share, rank), 'rows', split_...  11.6 us
  transfers between devices with their start and end apart: 23, of which 10 were waited for; matrix products, arithmetic and copies ran while one was open for 4% of the time, Pallas kernels for 10%

commit v1 on v0

--- a/solution.py
+++ b/solution.py
@@ -22,7 +22,7 @@
 GROUP = 8
 CHUNK = 6
 LAB_CHUNK = 8
-SIDE = 4
+SIDE = 5
 PASS_TYPES = (f32, bf16)
 
 
@@ -270,14 +270,14 @@
     lax.fori_loop(0, batches, end, 0)
 
 
-def pass_kernel(
-    slots, meta_ref, work_ref, w_ref, kept_any, turned_any, y_ref, out_ref, v_ref, t_ref, acc, v_sem, t_sem
-):
+def pass_kernel(slots, meta_ref, work_ref, ws_any, kept_any, turned_any, y_ref, out_ref, *refs):
+    w_ref, v_ref, t_ref, acc, w_sem, v_sem, t_sem = refs
     batches = (meta_ref[0, slots + y_ref.shape[0]] + GROUP - 1) // GROUP
 
     def copies(c):
         at = pl.ds(c * GROUP, GROUP)
         return (
+            pltpu.make_async_copy(ws_any.at[at], w_ref.at[at], w_sem.at[c]),
             pltpu.make_async_copy(turned_any.at[at], t_ref.at[at], t_sem.at[c]),
             pltpu.make_async_copy(kept_any.at[at], v_ref.at[at], v_sem.at[c]),
         )
@@ -393,7 +393,7 @@
             pltpu.make_async_copy(ref, f_ref.at[to], f_sem.at[k]).start()
     for k, copy in enumerate(t_copies):
         copy.wait()
-        table[k : k + 1] = coded[k, 0:1].astype(f32).astype(jnp.int32)
+        table[k : k + 1] = coded[k].astype(f32).astype(jnp.int32)[0:1]
     m_copy = pltpu.make_async_copy(table, meta_ref, m_sem)
     m_copy.start()
     acc[...] = jnp.zeros_like(acc)
@@ -565,6 +565,7 @@
     )
     pieces = [jnp.stack([same[h], other[h]]) for h in range(1, rows // 2)]
     pieces = [swap(piece, 2 * h) for h, piece in enumerate(pieces, 1)]
+    own_labs = jnp.concatenate([own, late_here[:, 0]], axis=1)
 
     def exchange(partial):
         partial = partial.reshape(patient_rows, rank)
@@ -623,12 +624,14 @@
         partial = pl.pallas_call(
             functools.partial(pass_kernel, slots),
             out_shape=shape_of((tiles, size, rank), PASS_TYPES[1]),
-            in_specs=[SMEM] * 2 + [VMEM, ANY, ANY, VMEM],
+            in_specs=[SMEM] * 2 + [ANY] * 3 + [VMEM],
             out_specs=VMEM,
             scratch_shapes=[
+                pltpu.VMEM((slots, size, size), bf16),
                 pltpu.VMEM((slots, size, rank), bf16),
                 pltpu.VMEM((slots, rank, size), bf16),
                 pltpu.VMEM((tiles, size, rank), f32),
+                pltpu.SemaphoreType.DMA((batches,)),
                 pltpu.SemaphoreType.DMA((batches,)),
                 pltpu.SemaphoreType.DMA((batches,)),
             ],
@@ -645,6 +648,7 @@
         )(iteration.reshape(1), exchange(partial), state, gram)
         return state, probe
 
+    own_labs, state, probe = lax.optimization_barrier((own_labs, state, probe))
     state, probe = lax.fori_loop(0, ITERS, turn, (state, probe))
     patient_out = state[0]
 
@@ -675,14 +679,13 @@
             pltpu.SemaphoreType.DMA((rows,)),
             pltpu.SemaphoreType.DMA,
         ],
-        compiler_params=params(BIG),
+        compiler_params=params(44),
         name="lab_step",
     )(row, same[0], other, *pieces, *factors, labs, late_here, late_there)
     back = lax.all_to_all(
         delta.reshape(col_tiles * lab_share, rank), "rows", split_axis=0, concat_axis=0, tiled=True
     )
     back = back.reshape(rows, owned_tiles, lab_share, rank).transpose(1, 0, 2, 3)
-    own_labs = jnp.concatenate([own, late_here[:, 0]], axis=1)
     updated = own_labs.reshape(owned_tiles, rows, lab_share, rank).astype(f32) + back.astype(f32)
     return (patient_out, updated.reshape(1, owned_tiles * size, rank))
 

time: 299 us -> 294 us (0.983); the launches traced: 300 us -> 289 us
  Pallas kernels: 54.1 us -> 49.4 us
  waiting for transfers between devices: 54.9 us -> 58.2 us
  transfers between devices with their start and end apart: 23 -> 23, of which waited for: 10 -> 9; matrix products, arithmetic and copies ran while one was open for 4% -> 4% of each run, Pallas kernels for 10% -> 10%
where the time goes in v1:
time: 294 us; the launch traced here: 289 us
  blocking collectives  86 us (29%)
  starting transfers between devices  66.6 us (23%)
  waiting for transfers between devices  58.2 us (20%)
  Pallas kernels  49.4 us (17%)
  between operations  14.9 us (5%)
  local copies, waits for them, and re-layouts  6.21 us (2%)
  other arithmetic  5.48 us (2%)
    all_to_all x4, blocking collectives, to_all(): lax.all_to_all(probe, 'cols', split_axis=0, concat_axis=0, tiled=True)  49 us
    ppermute x17, starting transfers between devices, swap(): return lax.ppermute(array, 'rows', [(i, i ^ k) for i in range(rows)])  46.7 us
    all_to_all x2, blocking collectives, to_columns(): lax.all_to_all(array, 'cols', split_axis=0, concat_axis=0, tiled=True)  37 us
    all_to_all x4, waiting for transfers between devices, exchange(): lax.all_to_all(partial, 'cols', split_axis=0, concat_axis=0, tiled=True)  33.7 us
    all_to_all x4, starting transfers between devices, exchange(): lax.all_to_all(partial, 'cols', split_axis=0, concat_axis=0, tiled=True)  16 us
    pallas_call x3, Pallas kernels, turn(): pl.pallas_call(functools.partial(pass_kernel, slots), out_shape=shape_of(...  14.8 us
    all_to_all x1, waiting for transfers between devices, shards(): lax.all_to_all(delta.reshape(col_tiles * lab_share, rank), 'rows', split_...  14.5 us
    pallas_call x1, Pallas kernels, shards(): pl.pallas_call(functools.partial(lab_kernel, slots, rows), out_shape=shap...  14.4 us
  transfers between devices with their start and end apart: 23, of which 9 were waited for; matrix products, arithmetic and copies ran while one was open for 4% of the time, Pallas kernels for 10%

profile of v1, /device:TPU:1, one launch (start us, length us, event | category | flops | bytes accessed | tf_op | source)
XLA Modules:
  0.0 289.1 jit_solution(3058085897306822573)
XLA Ops:
  7.2 0.0 copy-start
  7.2 0.0 all-gather.2.cloned.1.call-start
  7.2 1.2 slice.36
  8.4 21.7 %all_to_all.58 = bf16[16,96,256]{2,1,0:T(8,128)(2,1)} all-to-all(bf16[16,96,256]{2,1,0:T(8,128)(2,1)S(1)} %slice.36), channel_id=1, replica_groups=mesh['rows'=8,'cols'=16] {'cols'}, dimensions={0} | all-to-all | bytes 1572864 | tf_op jit(solution)/shard_map/all_to_all | solution.py:512
  30.1 0.0 all-gather.2.cloned.1.call-update
  30.2 1.0 slice.37
  31.1 1.4 collective-permute-start
  32.5 2.6 collective-permute-start.1
  35.8 11.3 %prep.1 = (s32[1,128]{1,0:T(1,128)S(1)}, s32[4,128]{1,0:T(4,128)S(1)}, bf16[64,128,128]{2,1,0:T(8,128)(2,1)}, bf16[64,128,128]{2,1,0:T(8,128)(2,1)}, bf16[129,16...) custom-call(s32[1]{0:T(128)} %bitcast.11.row_ref, ...), custom_call_target="tpu_custom_call" | custom-call | flops 1000000000 | bytes 50331648 | tf_op jit(solution)/shard_map/prep/pallas_call | solution.py:517
  47.1 2.6 collective-permute-start.4
  49.7 0.1 pad_maximum_fusion.3
  49.9 15.3 %all_to_all.59.here_any.refs_14_ = bf16[16,4,32,256]{3,2,1,0:T(8,128)(2,1)S(1)} all-to-all(bf16[16,4,32,256]{3,2,1,0:T(8,128)(2,1)S(1)} %pad_maximum_fusion.3), channel_id=1, replica_groups=mesh['rows'=8,'cols'=16] {'cols'}, dimensions={0} | all-to-all | bytes 2097152 | tf_op jit(solution)/shard_map/all_to_all | solution.py:512
  65.1 6.2 %collective-permute-start.3 = (bf16[16,4,32,256]{3,2,1,0:T(8,128)(2,1)S(1)}, bf16[16,4,32,256]{3,2,1,0:T(8,128)(2,1)S(1)}, u32[]{:S(2)}, u32[]{:S(2)}) collective-permute-start(bf16[16,4,32,256]{3,2,1,0:T(8,128)(2,1)S(1)} %all_to_all.59.here_any.refs_14_), channel_id=1, source_target_pairs={{0,16},{16,0},{32,48},{48,32},{64,80},{80,64},{96,112},{112,96},{1... | collective-permute-start | bytes 3145736 | tf_op jit(solution)/shard_map/ppermute | solution.py:509
  71.3 0.8 dynamic-slice_convert_fusion.start_ref
  72.1 0.9 convolution_subtract_fusion.1
  73.0 1.0 convolution_subtract_fusion.side_ref
  74.0 0.2 fusion.4.gram_ref
  74.3 3.2 %all-gather.2.cloned.1.call-done.early_any.refs_13_ = bf16[128,96,256]{2,1,0:T(8,128)(2,1)} async-done(((bf16[16,96,256]{2,1,0:T(8,128)(2,1)}), bf16[128,96,256]{2,1,0:T(8,128)(2,1)}) %all-gather.2.cloned.1.call-update) | async-done | bytes 6291472 | tf_op jit(solution)/shard_map/all_gather | solution.py:543
  77.5 7.3 %first_pass.1 = (f32[8,128,256]{2,1,0:T(8,128)}, bf16[64,128,256]{2,1,0:T(8,128)(2,1)}, bf16[64,256,128]{2,1,0:T(8,128)(2,1)}) custom-call(s32[1]{0:T(128)} %bitcast.11.row_ref, s32[1,128]{1,0:T(1,128)S(1)} %get-tuple-element.291.meta_ref, s32[4,128]{1,0:T(4,128)S(1)} %get-tuple-element.292.work_ref, bf16[64,128,128]{2,1,0:T(8,128)(2,1)} %get-tuple-element.189.xs_any, ...), custom_call_target="tpu_custom_call" | custom-call | tf_op jit(solution)/shard_map/first_pass/pallas_call | solution.py:583
  84.8 4.0 %all-to-all-start.4 = ((f32[16,64,256]{2,1,0:T(8,128)}), f32[16,64,256]{2,1,0:T(8,128)S(1)}, u32[]{:S(2)}, u32[]{:S(2)}) async-start(f32[16,64,256]{2,1,0:T(8,128)} %bitcast.60), calls=%async_computation.4 | async-start | bytes 2097152 | tf_op jit(solution)/shard_map/all_to_all | solution.py:572
  88.8 1.7 fusion.3
  90.6 1.1 pad_maximum_fusion
  91.6 1.1 pad_maximum_fusion.1
  92.7 1.8 collective-permute-start.6
  94.5 1.1 pad_maximum_fusion.2
  95.6 2.1 collective-permute-start.7
  97.7 1.1 pad_maximum_fusion.4
  98.7 6.9 %all-to-all-done.4.recv_ref = f32[16,64,256]{2,1,0:T(8,128)S(1)} async-done(((f32[16,64,256]{2,1,0:T(8,128)}), f32[16,64,256]{2,1,0:T(8,128)S(1)}, u32[]{:S(2)}, u32[]{:S(2)}) %all-to-all-start.4) | async-done | bytes 1048608 | tf_op jit(solution)/shard_map/all_to_all | solution.py:572
  105.7 0.3 first_step.1
  106.0 91.9 %while.15 = (s32[]{:T(128)}, f32[4,64,256]{2,1,0:T(8,128)S(1)}, bf16[16,64,256]{2,1,0:T(8,128)(2,1)S(1)}, s32[1,128]{1,0:T(1,128)S(1)}, s32[4,128]{1,0:T(4,128)S...) while((s32[]{:T(128)}, f32[4,64,256]{2,1,0:T(8,128)S(1)}, ...), condition=%wide.region_1.0_spmd, body=%wide.region_0.0_spmd.sunk | while | flops 2 | bytes 3145869 | solution.py:652
  106.0 12.6 %all_to_all.61 = bf16[16,64,256]{2,1,0:T(8,128)(2,1)S(1)} all-to-all(bf16[16,64,256]{2,1,0:T(8,128)(2,1)S(1)} %get-tuple-element.300), channel_id=1, replica_groups=mesh['rows'=8,'cols'=16] {'cols'}, dimensions={0} | all-to-all | bytes 1048576 | tf_op jit(solution)/shard_map/while/body/eval_jaxpr/all_to_all | solution.py:577
  118.7 4.9 %patient_pass.5 = bf16[8,128,256]{2,1,0:T(8,128)(2,1)} custom-call(s32[1,128]{1,0:T(1,128)S(1)} %get-tuple-element.311.meta_ref, s32[4,128]{1,0:T(4,128)S(1)} %get-tuple-element.312.work_ref, bf16[64,128,128]{2,1,0:T(8,128)(2,1)} %get-tuple-element.313.ws_any, bf16[64,128,256]{2,1,0:T(8,128)(2,1)} %get-tuple-element.314.kept_any, ...), custom_call_target="tpu_custom_call" | custom-call | tf_op jit(solution)/shard_map/while/body/eval_jaxpr/patient_pass/pallas_call | solution.py:624
  123.6 4.4 %all-to-all-start.1 = ((bf16[16,64,256]{2,1,0:T(8,128)(2,1)}), bf16[16,64,256]{2,1,0:T(8,128)(2,1)S(1)}, u32[]{:S(2)}, u32[]{:S(2)}) async-start(bf16[16,64,256]{2,1,0:T(8,128)(2,1)} %bitcast.47), calls=%async_computation.1 | async-start | bytes 1048576 | tf_op jit(solution)/shard_map/while/body/eval_jaxpr/all_to_all | solution.py:572
  128.0 8.9 %all-to-all-done.1.recv_ref = bf16[16,64,256]{2,1,0:T(8,128)(2,1)S(1)} async-done(((bf16[16,64,256]{2,1,0:T(8,128)(2,1)}), bf16[16,64,256]{2,1,0:T(8,128)(2,1)S(1)}, u32[]{:S(2)}, u32[]{:S(2)}) %all-to-all-start.1) | async-done | bytes 524320 | tf_op jit(solution)/shard_map/while/body/eval_jaxpr/all_to_all | solution.py:572
  137.0 0.5 step.5
  137.5 12.4 %all_to_all.61 = bf16[16,64,256]{2,1,0:T(8,128)(2,1)S(1)} all-to-all(bf16[16,64,256]{2,1,0:T(8,128)(2,1)S(1)} %get-tuple-element.300), channel_id=1, replica_groups=mesh['rows'=8,'cols'=16] {'cols'}, dimensions={0} | all-to-all | bytes 1048576 | tf_op jit(solution)/shard_map/while/body/eval_jaxpr/all_to_all | solution.py:577
  149.9 4.9 %patient_pass.5 = bf16[8,128,256]{2,1,0:T(8,128)(2,1)} custom-call(s32[1,128]{1,0:T(1,128)S(1)} %get-tuple-element.311.meta_ref, s32[4,128]{1,0:T(4,128)S(1)} %get-tuple-element.312.work_ref, bf16[64,128,128]{2,1,0:T(8,128)(2,1)} %get-tuple-element.313.ws_any, bf16[64,128,256]{2,1,0:T(8,128)(2,1)} %get-tuple-element.314.kept_any, ...), custom_call_target="tpu_custom_call" | custom-call | tf_op jit(solution)/shard_map/while/body/eval_jaxpr/patient_pass/pallas_call | solution.py:624
  154.8 3.8 %all-to-all-start.1 = ((bf16[16,64,256]{2,1,0:T(8,128)(2,1)}), bf16[16,64,256]{2,1,0:T(8,128)(2,1)S(1)}, u32[]{:S(2)}, u32[]{:S(2)}) async-start(bf16[16,64,256]{2,1,0:T(8,128)(2,1)} %bitcast.47), calls=%async_computation.1 | async-start | bytes 1048576 | tf_op jit(solution)/shard_map/while/body/eval_jaxpr/all_to_all | solution.py:572
  158.7 8.9 %all-to-all-done.1.recv_ref = bf16[16,64,256]{2,1,0:T(8,128)(2,1)S(1)} async-done(((bf16[16,64,256]{2,1,0:T(8,128)(2,1)}), bf16[16,64,256]{2,1,0:T(8,128)(2,1)S(1)}, u32[]{:S(2)}, u32[]{:S(2)}) %all-to-all-start.1) | async-done | bytes 524320 | tf_op jit(solution)/shard_map/while/body/eval_jaxpr/all_to_all | solution.py:572
  167.6 0.5 step.5
  168.1 11.9 %all_to_all.61 = bf16[16,64,256]{2,1,0:T(8,128)(2,1)S(1)} all-to-all(bf16[16,64,256]{2,1,0:T(8,128)(2,1)S(1)} %get-tuple-element.300), channel_id=1, replica_groups=mesh['rows'=8,'cols'=16] {'cols'}, dimensions={0} | all-to-all | bytes 1048576 | tf_op jit(solution)/shard_map/while/body/eval_jaxpr/all_to_all | solution.py:577
  180.0 4.9 %patient_pass.5 = bf16[8,128,256]{2,1,0:T(8,128)(2,1)} custom-call(s32[1,128]{1,0:T(1,128)S(1)} %get-tuple-element.311.meta_ref, s32[4,128]{1,0:T(4,128)S(1)} %get-tuple-element.312.work_ref, bf16[64,128,128]{2,1,0:T(8,128)(2,1)} %get-tuple-element.313.ws_any, bf16[64,128,256]{2,1,0:T(8,128)(2,1)} %get-tuple-element.314.kept_any, ...), custom_call_target="tpu_custom_call" | custom-call | tf_op jit(solution)/shard_map/while/body/eval_jaxpr/patient_pass/pallas_call | solution.py:624
  185.0 3.8 %all-to-all-start.1 = ((bf16[16,64,256]{2,1,0:T(8,128)(2,1)}), bf16[16,64,256]{2,1,0:T(8,128)(2,1)S(1)}, u32[]{:S(2)}, u32[]{:S(2)}) async-start(bf16[16,64,256]{2,1,0:T(8,128)(2,1)} %bitcast.47), calls=%async_computation.1 | async-start | bytes 1048576 | tf_op jit(solution)/shard_map/while/body/eval_jaxpr/all_to_all | solution.py:572
  188.8 8.9 %all-to-all-done.1.recv_ref = bf16[16,64,256]{2,1,0:T(8,128)(2,1)S(1)} async-done(((bf16[16,64,256]{2,1,0:T(8,128)(2,1)}), bf16[16,64,256]{2,1,0:T(8,128)(2,1)S(1)}, u32[]{:S(2)}, u32[]{:S(2)}) %all-to-all-start.1) | async-done | bytes 524320 | tf_op jit(solution)/shard_map/while/body/eval_jaxpr/all_to_all | solution.py:572
  197.7 0.2 step.5
  198.0 12.0 %all_to_all.60 = bf16[16,64,256]{2,1,0:T(8,128)(2,1)S(1)} all-to-all(bf16[16,64,256]{2,1,0:T(8,128)(2,1)S(1)} %get-tuple-element.207), channel_id=1, replica_groups=mesh['rows'=8,'cols'=16] {'cols'}, dimensions={0} | all-to-all | bytes 1048576 | tf_op jit(solution)/shard_map/all_to_all | solution.py:577
  210.0 1.1 collective-permute-start.9
  211.1 9.8 %collective-permute-start.8 = (bf16[8,128,256]{2,1,0:T(8,128)(2,1)S(1)}, bf16[8,128,256]{2,1,0:T(8,128)(2,1)S(1)}, u32[]{:S(2)}, u32[]{:S(2)}) collective-permute-start(bf16[8,128,256]{2,1,0:T(8,128)(2,1)S(1)} %bitcast.50), channel_id=1, source_target_pairs={{0,32},{16,48},{32,0},{48,16},{64,96},{80,112},{96,64},{112,80},{1... | collective-permute-start | bytes 1572872 | tf_op jit(solution)/shard_map/ppermute | solution.py:509
  221.0 9.7 %collective-permute-start.12 = (bf16[8,128,256]{2,1,0:T(8,128)(2,1)S(1)}, bf16[8,128,256]{2,1,0:T(8,128)(2,1)S(1)}, u32[]{:S(2)}, u32[]{:S(2)}) collective-permute-start(bf16[8,128,256]{2,1,0:T(8,128)(2,1)S(1)} %bitcast.51), channel_id=1, source_target_pairs={{0,16},{16,0},{32,48},{48,32},{64,80},{80,64},{96,112},{112,96},{1... | collective-permute-start | bytes 1572872 | tf_op jit(solution)/shard_map/ppermute | solution.py:509
  230.7 3.2 %collective-permute-start.10 = (bf16[4,128,256]{2,1,0:T(8,128)(2,1)S(1)}, bf16[4,128,256]{2,1,0:T(8,128)(2,1)S(1)}, u32[]{:S(2)}, u32[]{:S(2)}) collective-permute-start(bf16[4,128,256]{2,1,0:T(8,128)(2,1)S(1)} %slice.38), channel_id=1, source_target_pairs={{0,32},{16,48},{32,0},{48,16},{64,96},{80,112},{96,64},{112,80},{1... | collective-permute-start | bytes 786440 | tf_op jit(solution)/shard_map/ppermute | solution.py:509
  234.0 1.7 collective-permute-start.13
  235.7 0.1 collective-permute-start.14
  235.8 0.8 collective-permute-start.11
  236.6 2.3 collective-permute-done.10.refs_6_
  238.9 2.3 collective-permute-start.15
  241.2 3.3 %collective-permute-done.11.refs_7_ = bf16[4,128,256]{2,1,0:T(8,128)(2,1)S(1)} collective-permute-done((bf16[4,128,256]{2,1,0:T(8,128)(2,1)S(1)}, bf16[4,128,256]{2,1,0:T(8,128)(2,1)S(1)}, u32[]{:S(2)}, u32[]{:S(2)}) %collective-permute-start.11) | collective-permute-done | bytes 262176 | tf_op jit(solution)/shard_map/ppermute | solution.py:509
  244.5 1.2 collective-permute-start.16
  245.7 1.1 collective-permute-done.16.refs_12_
  246.9 14.4 %lab_step.1 = bf16[128,16,256]{2,1,0:T(8,128)(2,1)} custom-call(s32[1]{0:T(128)} %bitcast.11.row_ref, bf16[129,16,128]{2,1,0:T(8,128)(2,1)S(1)} %copy-done.5, bf16[4,129,16,128]{3,2,1,0:T(8,128)(2,1)} %collective-permute-done.4.other_any, bf16[2,129,16,128]{3,2,1,0:T(8,128)(2,1)} %collective-permute-done.5.refs_0_, ...), custom_call_target="tpu_custom_call" | custom-call | tf_op jit(solution)/shard_map/lab_step/pallas_call | solution.py:661
  261.3 4.0 %all-to-all-start.6 = ((bf16[8,256,256]{2,1,0:T(8,128)(2,1)}), bf16[8,256,256]{2,1,0:T(8,128)(2,1)S(1)}, u32[]{:S(2)}, u32[]{:S(2)}) async-start(bf16[8,256,256]{2,1,0:T(8,128)(2,1)} %bitcast.23), calls=%async_computation.6 | async-start | bytes 2097152 | tf_op jit(solution)/shard_map/all_to_all | solution.py:685
  265.3 0.6 slice_bitcast_fusion.1
  265.9 14.5 %all-to-all-done.6 = bf16[8,256,256]{2,1,0:T(8,128)(2,1)S(1)} async-done(((bf16[8,256,256]{2,1,0:T(8,128)(2,1)}), bf16[8,256,256]{2,1,0:T(8,128)(2,1)S(1)}, u32[]{:S(2)}, u32[]{:S(2)}) %all-to-all-start.6) | async-done | bytes 1048608 | tf_op jit(solution)/shard_map/all_to_all | solution.py:685
  280.4 0.3 fusion
  280.7 1.5 copy.27
  (43 shorter events, 0.2 us)
Async XLA Ops:
  7.2 64.9 %copy-start = (bf16[256,256]{1,0:T(8,128)(2,1)S(1)}, bf16[256,256]{1,0:T(8,128)(2,1)}, u32[]{:S(2)}) copy-start(bf16[256,256]{1,0:T(8,128)(2,1)} %param.19) | copy-start | bytes 393220
  7.2 70.3 %all-gather.2.cloned.1.call-start = ((), (), s32[]{:S(2)}) async-start(), calls=%async_computation.7 | async-start | bytes 7077888 | tf_op jit(solution)/shard_map/all_gather | solution.py:543
  31.1 18.6 %collective-permute-start = (bf16[16,32,256]{2,1,0:T(8,128)(2,1)S(1)}, bf16[16,32,256]{2,1,0:T(8,128)(2,1)S(1)}, u32[]{:S(2)}, u32[]{:S(2)}) collective-permute-start(bf16[16,32,256]{2,1,0:T(8,128)(2,1)S(1)} %slice.37), channel_id=1, source_target_pairs={{0,32},{16,48},{32,0},{48,16},{64,96},{80,112},{96,64},{112,80},{1... | collective-permute-start | bytes 786440 | tf_op jit(solution)/shard_map/ppermute | solution.py:509
  32.5 17.2 %collective-permute-start.1 = (bf16[16,32,256]{2,1,0:T(8,128)(2,1)S(1)}, bf16[16,32,256]{2,1,0:T(8,128)(2,1)S(1)}, u32[]{:S(2)}, u32[]{:S(2)}) collective-permute-start(bf16[16,32,256]{2,1,0:T(8,128)(2,1)S(1)} %slice.37), channel_id=1, source_target_pairs={{0,64},{16,80},{32,96},{48,112},{64,0},{80,16},{96,32},{112,48},{1... | collective-permute-start | bytes 786440 | tf_op jit(solution)/shard_map/ppermute | solution.py:509
  35.1 14.6 %collective-permute-start.2 = (bf16[16,32,256]{2,1,0:T(8,128)(2,1)S(1)}, bf16[16,32,256]{2,1,0:T(8,128)(2,1)S(1)}, u32[]{:S(2)}, u32[]{:S(2)}) collective-permute-start(bf16[16,32,256]{2,1,0:T(8,128)(2,1)S(1)} %slice.37), channel_id=1, source_target_pairs={{0,96},{16,112},{32,64},{48,80},{64,32},{80,48},{96,0},{112,16},{1... | collective-permute-start | bytes 786440 | tf_op jit(solution)/shard_map/ppermute | solution.py:509
  47.1 27.1 %collective-permute-start.4 = (bf16[4,129,16,128]{3,2,1,0:T(8,128)(2,1)}, bf16[4,129,16,128]{3,2,1,0:T(8,128)(2,1)}, u32[]{:S(2)}, u32[]{:S(2)}) collective-permute-start(bf16[4,129,16,128]{3,2,1,0:T(8,128)(2,1)} %get-tuple-element.185), channel_id=1, source_target_pairs={{0,16},{16,0},{32,48},{48,32},{64,80},{80,64},{96,112},{112,96},{1... | collective-permute-start | bytes 6340616 | tf_op jit(solution)/shard_map/ppermute | solution.py:509
  65.1 12.3 %copy-start.1 = (bf16[16,4,32,256]{3,2,1,0:T(8,128)(2,1)}, bf16[16,4,32,256]{3,2,1,0:T(8,128)(2,1)S(1)}, u32[]{:S(2)}) copy-start(bf16[16,4,32,256]{3,2,1,0:T(8,128)(2,1)S(1)} %all_to_all.59.here_any.refs_14_) | copy-start | bytes 3145732
  65.1 9.1 %collective-permute-start.3 = (bf16[16,4,32,256]{3,2,1,0:T(8,128)(2,1)S(1)}, bf16[16,4,32,256]{3,2,1,0:T(8,128)(2,1)S(1)}, u32[]{:S(2)}, u32[]{:S(2)}) collective-permute-start(bf16[16,4,32,256]{3,2,1,0:T(8,128)(2,1)S(1)} %all_to_all.59.here_any.refs_14_), channel_id=1, source_target_pairs={{0,16},{16,0},{32,48},{48,32},{64,80},{80,64},{96,112},{112,96},{1... | collective-permute-start | bytes 3145736 | tf_op jit(solution)/shard_map/ppermute | solution.py:509
  74.2 3.2 %copy-start.3 = (bf16[16,4,32,256]{3,2,1,0:T(8,128)(2,1)}, bf16[16,4,32,256]{3,2,1,0:T(8,128)(2,1)S(1)}, u32[]{:S(2)}) copy-start(bf16[16,4,32,256]{3,2,1,0:T(8,128)(2,1)S(1)} %collective-permute-done.3.there_any.refs_15_) | copy-start | bytes 3145732
  84.8 20.9 %all-to-all-start.4 = ((f32[16,64,256]{2,1,0:T(8,128)}), f32[16,64,256]{2,1,0:T(8,128)S(1)}, u32[]{:S(2)}, u32[]{:S(2)}) async-start(f32[16,64,256]{2,1,0:T(8,128)} %bitcast.60), calls=%async_computation.4 | async-start | bytes 2097152 | tf_op jit(solution)/shard_map/all_to_all | solution.py:572
  88.8 1.7 copy-start.10
  88.8 2.8 copy-start.9
  90.6 3.9 %copy-start.8 = (bf16[129,16,128]{2,1,0:T(8,128)(2,1)S(1)}, bf16[129,16,128]{2,1,0:T(8,128)(2,1)}, u32[]{:S(2)}) copy-start(bf16[129,16,128]{2,1,0:T(8,128)(2,1)} %get-tuple-element.206) | copy-start | bytes 1585156
  91.6 142.3 %collective-permute-start.5 = (bf16[2,129,16,128]{3,2,1,0:T(8,128)(2,1)}, bf16[2,129,16,128]{3,2,1,0:T(8,128)(2,1)}, u32[]{:S(2)}, u32[]{:S(2)}) collective-permute-start(bf16[2,129,16,128]{3,2,1,0:T(8,128)(2,1)} %pad_maximum_fusion), channel_id=1, source_target_pairs={{0,32},{16,48},{32,0},{48,16},{64,96},{80,112},{96,64},{112,80},{1... | collective-permute-start | bytes 3170312 | tf_op jit(solution)/shard_map/ppermute | solution.py:509
  91.6 6.0 %copy-start.2 = (bf16[16,4,32,256]{3,2,1,0:T(8,128)(2,1)S(1)}, bf16[16,4,32,256]{3,2,1,0:T(8,128)(2,1)}, u32[]{:S(2)}) copy-start(bf16[16,4,32,256]{3,2,1,0:T(8,128)(2,1)} %copy-done.1) | copy-start | bytes 3145732
  91.6 6.0 %copy-start.6 = (bf16[16,96,256]{2,1,0:T(8,128)(2,1)S(1)}, bf16[16,96,256]{2,1,0:T(8,128)(2,1)}, u32[]{:S(2)}) copy-start(bf16[16,96,256]{2,1,0:T(8,128)(2,1)} %all_to_all.58) | copy-start | bytes 2359300
  92.7 143.0 %collective-permute-start.6 = (bf16[2,129,16,128]{3,2,1,0:T(8,128)(2,1)}, bf16[2,129,16,128]{3,2,1,0:T(8,128)(2,1)}, u32[]{:S(2)}, u32[]{:S(2)}) collective-permute-start(bf16[2,129,16,128]{3,2,1,0:T(8,128)(2,1)} %pad_maximum_fusion.1), channel_id=1, source_target_pairs={{0,64},{16,80},{32,96},{48,112},{64,0},{80,16},{96,32},{112,48},{1... | collective-permute-start | bytes 3170312 | tf_op jit(solution)/shard_map/ppermute | solution.py:509
  95.6 140.2 %collective-permute-start.7 = (bf16[2,129,16,128]{3,2,1,0:T(8,128)(2,1)}, bf16[2,129,16,128]{3,2,1,0:T(8,128)(2,1)}, u32[]{:S(2)}, u32[]{:S(2)}) collective-permute-start(bf16[2,129,16,128]{3,2,1,0:T(8,128)(2,1)} %pad_maximum_fusion.2), channel_id=1, source_target_pairs={{0,96},{16,112},{32,64},{48,80},{64,32},{80,48},{96,0},{112,16},{1... | collective-permute-start | bytes 3170312 | tf_op jit(solution)/shard_map/ppermute | solution.py:509
  123.6 13.3 %all-to-all-start.1 = ((bf16[16,64,256]{2,1,0:T(8,128)(2,1)}), bf16[16,64,256]{2,1,0:T(8,128)(2,1)S(1)}, u32[]{:S(2)}, u32[]{:S(2)}) async-start(bf16[16,64,256]{2,1,0:T(8,128)(2,1)} %bitcast.47), calls=%async_computation.1 | async-start | bytes 1048576 | tf_op jit(solution)/shard_map/while/body/eval_jaxpr/all_to_all | solution.py:572
  154.8 12.7 %all-to-all-start.1 = ((bf16[16,64,256]{2,1,0:T(8,128)(2,1)}), bf16[16,64,256]{2,1,0:T(8,128)(2,1)S(1)}, u32[]{:S(2)}, u32[]{:S(2)}) async-start(bf16[16,64,256]{2,1,0:T(8,128)(2,1)} %bitcast.47), calls=%async_computation.1 | async-start | bytes 1048576 | tf_op jit(solution)/shard_map/while/body/eval_jaxpr/all_to_all | solution.py:572
  185.0 12.7 %all-to-all-start.1 = ((bf16[16,64,256]{2,1,0:T(8,128)(2,1)}), bf16[16,64,256]{2,1,0:T(8,128)(2,1)S(1)}, u32[]{:S(2)}, u32[]{:S(2)}) async-start(bf16[16,64,256]{2,1,0:T(8,128)(2,1)} %bitcast.47), calls=%async_computation.1 | async-start | bytes 1048576 | tf_op jit(solution)/shard_map/while/body/eval_jaxpr/all_to_all | solution.py:572
  198.0 48.9 %copy-start.4 = (bf16[16,4,32,256]{3,2,1,0:T(8,128)(2,1)S(1)}, bf16[16,4,32,256]{3,2,1,0:T(8,128)(2,1)}, u32[]{:S(2)}) copy-start(bf16[16,4,32,256]{3,2,1,0:T(8,128)(2,1)} %copy-done.3) | copy-start | bytes 3145732
  198.0 48.9 %copy-start.5 = (bf16[129,16,128]{2,1,0:T(8,128)(2,1)S(1)}, bf16[129,16,128]{2,1,0:T(8,128)(2,1)}, u32[]{:S(2)}) copy-start(bf16[129,16,128]{2,1,0:T(8,128)(2,1)} %get-tuple-element.202.same_any) | copy-start | bytes 1585156
  210.0 10.9 %collective-permute-start.9 = (bf16[8,128,256]{2,1,0:T(8,128)(2,1)S(1)}, bf16[8,128,256]{2,1,0:T(8,128)(2,1)S(1)}, u32[]{:S(2)}, u32[]{:S(2)}) collective-permute-start(bf16[8,128,256]{2,1,0:T(8,128)(2,1)S(1)} %bitcast.49), channel_id=1, source_target_pairs={{0,96},{16,112},{32,64},{48,80},{64,32},{80,48},{96,0},{112,16},{1... | collective-permute-start | bytes 1572872 | tf_op jit(solution)/shard_map/ppermute | solution.py:509
  211.1 19.6 %collective-permute-start.8 = (bf16[8,128,256]{2,1,0:T(8,128)(2,1)S(1)}, bf16[8,128,256]{2,1,0:T(8,128)(2,1)S(1)}, u32[]{:S(2)}, u32[]{:S(2)}) collective-permute-start(bf16[8,128,256]{2,1,0:T(8,128)(2,1)S(1)} %bitcast.50), channel_id=1, source_target_pairs={{0,32},{16,48},{32,0},{48,16},{64,96},{80,112},{96,64},{112,80},{1... | collective-permute-start | bytes 1572872 | tf_op jit(solution)/shard_map/ppermute | solution.py:509
  221.0 24.8 %collective-permute-start.12 = (bf16[8,128,256]{2,1,0:T(8,128)(2,1)S(1)}, bf16[8,128,256]{2,1,0:T(8,128)(2,1)S(1)}, u32[]{:S(2)}, u32[]{:S(2)}) collective-permute-start(bf16[8,128,256]{2,1,0:T(8,128)(2,1)S(1)} %bitcast.51), channel_id=1, source_target_pairs={{0,16},{16,0},{32,48},{48,32},{64,80},{80,64},{96,112},{112,96},{1... | collective-permute-start | bytes 1572872 | tf_op jit(solution)/shard_map/ppermute | solution.py:509
  230.7 8.2 %collective-permute-start.10 = (bf16[4,128,256]{2,1,0:T(8,128)(2,1)S(1)}, bf16[4,128,256]{2,1,0:T(8,128)(2,1)S(1)}, u32[]{:S(2)}, u32[]{:S(2)}) collective-permute-start(bf16[4,128,256]{2,1,0:T(8,128)(2,1)S(1)} %slice.38), channel_id=1, source_target_pairs={{0,32},{16,48},{32,0},{48,16},{64,96},{80,112},{96,64},{112,80},{1... | collective-permute-start | bytes 786440 | tf_op jit(solution)/shard_map/ppermute | solution.py:509
  234.0 11.8 %collective-permute-start.13 = (bf16[8,128,256]{2,1,0:T(8,128)(2,1)S(1)}, bf16[8,128,256]{2,1,0:T(8,128)(2,1)S(1)}, u32[]{:S(2)}, u32[]{:S(2)}) collective-permute-start(bf16[8,128,256]{2,1,0:T(8,128)(2,1)S(1)} %collective-permute-done.8.refs_4_), channel_id=1, source_target_pairs={{0,16},{16,0},{32,48},{48,32},{64,80},{80,64},{96,112},{112,96},{1... | collective-permute-start | bytes 1572872 | tf_op jit(solution)/shard_map/ppermute | solution.py:509
  235.7 10.0 %collective-permute-start.14 = (bf16[8,128,256]{2,1,0:T(8,128)(2,1)S(1)}, bf16[8,128,256]{2,1,0:T(8,128)(2,1)S(1)}, u32[]{:S(2)}, u32[]{:S(2)}) collective-permute-start(bf16[8,128,256]{2,1,0:T(8,128)(2,1)S(1)} %collective-permute-done.9.refs_5_), channel_id=1, source_target_pairs={{0,16},{16,0},{32,48},{48,32},{64,80},{80,64},{96,112},{112,96},{1... | collective-permute-start | bytes 1572872 | tf_op jit(solution)/shard_map/ppermute | solution.py:509
  235.8 8.7 %collective-permute-start.11 = (bf16[4,128,256]{2,1,0:T(8,128)(2,1)S(1)}, bf16[4,128,256]{2,1,0:T(8,128)(2,1)S(1)}, u32[]{:S(2)}, u32[]{:S(2)}) collective-permute-start(bf16[4,128,256]{2,1,0:T(8,128)(2,1)S(1)} %slice.39), channel_id=1, source_target_pairs={{0,96},{16,112},{32,64},{48,80},{64,32},{80,48},{96,0},{112,16},{1... | collective-permute-start | bytes 786440 | tf_op jit(solution)/shard_map/ppermute | solution.py:509
  238.9 6.8 %collective-permute-start.15 = (bf16[4,128,256]{2,1,0:T(8,128)(2,1)S(1)}, bf16[4,128,256]{2,1,0:T(8,128)(2,1)S(1)}, u32[]{:S(2)}, u32[]{:S(2)}) collective-permute-start(bf16[4,128,256]{2,1,0:T(8,128)(2,1)S(1)} %collective-permute-done.10.refs_6_), channel_id=1, source_target_pairs={{0,16},{16,0},{32,48},{48,32},{64,80},{80,64},{96,112},{112,96},{1... | collective-permute-start | bytes 786440 | tf_op jit(solution)/shard_map/ppermute | solution.py:509
  244.5 2.4 collective-permute-start.16
  261.3 19.1 %copy-start.7 = (bf16[16,128,256]{2,1,0:T(8,128)(2,1)S(1)}, bf16[16,128,256]{2,1,0:T(8,128)(2,1)}, u32[]{:S(2)}) copy-start(bf16[16,128,256]{2,1,0:T(8,128)(2,1)} %pad_maximum_fusion.4) | copy-start | bytes 3145732
  261.3 19.1 %all-to-all-start.6 = ((bf16[8,256,256]{2,1,0:T(8,128)(2,1)}), bf16[8,256,256]{2,1,0:T(8,128)(2,1)S(1)}, u32[]{:S(2)}, u32[]{:S(2)}) async-start(bf16[8,256,256]{2,1,0:T(8,128)(2,1)} %bitcast.23), calls=%async_computation.6 | async-start | bytes 2097152 | tf_op jit(solution)/shard_map/all_to_all | solution.py:685
Sparse Core Ops, SparseCore 0:
  30.3 47.1 all-gather.1

commit v2 on v1

--- a/solution.py
+++ b/solution.py
@@ -163,7 +163,6 @@
 
 
 def patient_sums(with_values, work_ref, x_ref, w_ref, v_ref, t_ref, y_ref, out_ref, acc, arrive):
-    acc[...] = jnp.zeros_like(acc)
 
     def chunk(c):
         tile, first, end = [work_ref[f, c] for f in range(3)]
@@ -253,6 +252,7 @@
             copy.start()
         return carry
 
+    acc[...] = jnp.zeros_like(acc)
     wait(0, 0)
 
     def arrive(there, hi):
@@ -293,6 +293,7 @@
         return carry
 
     lax.fori_loop(0, batches, start, 0)
+    acc[...] = jnp.zeros_like(acc)
     wait(0, 0)
 
     def arrive(there, hi):
@@ -391,12 +392,12 @@
         for h, ref in enumerate(factors[k]):
             to = pl.ds((row ^ k) * tiles + h * half, ref.shape[0])
             pltpu.make_async_copy(ref, f_ref.at[to], f_sem.at[k]).start()
+    acc[...] = jnp.zeros_like(acc)
     for k, copy in enumerate(t_copies):
         copy.wait()
         table[k : k + 1] = coded[k].astype(f32).astype(jnp.int32)[0:1]
     m_copy = pltpu.make_async_copy(table, meta_ref, m_sem)
     m_copy.start()
-    acc[...] = jnp.zeros_like(acc)
     curv[...] = jnp.zeros_like(curv)
     m_copy.wait()
     pltpu.make_async_copy(v_ref, v_ref, v_sem).wait()

time: 294 us -> 295 us (level); the launches traced: 289 us -> 296 us
  waiting for transfers between devices: 58.2 us -> 66.4 us
  starting transfers between devices: 66.6 us -> 58.8 us
  Pallas kernels: 49.4 us -> 53.6 us
    ppermute x17, starting transfers between devices: 46.7 us -> 35.7 us  [swap(): return lax.ppermute(array, 'rows', [(i, i ^ k) for i in range(rows)])]
    ppermute x17, waiting for transfers between devices: 6.74 us -> 16.6 us  [swap(): return lax.ppermute(array, 'rows', [(i, i ^ k) for i in range(rows)])]
    pallas_call x1, Pallas kernels: 14.4 us -> 19.1 us  [shards(): pl.pallas_call(functools.partial(lab_kernel, slots, rows), out_shape=shap...]
    all_to_all x4, starting transfers between devices: 16 us -> 19.1 us  [exchange(): lax.all_to_all(partial, 'cols', split_axis=0, concat_axis=0, tiled=True)]
  transfers between devices with their start and end apart: 23 -> 23, of which waited for: 9 -> 10; matrix products, arithmetic and copies ran while one was open for 4% -> 4% of each run, Pallas kernels for 10% -> 9%
where the time goes in v2:
time: 295 us; the launch traced here: 296 us
  blocking collectives  88 us (30%)
  waiting for transfers between devices  66.4 us (23%)
  starting transfers between devices  58.8 us (20%)
  Pallas kernels  53.6 us (18%)
  between operations  15 us (5%)
  local copies, waits for them, and re-layouts  6.21 us (2%)
  other arithmetic  5.48 us (2%)
    all_to_all x4, blocking collectives, to_all(): lax.all_to_all(probe, 'cols', split_axis=0, concat_axis=0, tiled=True)  51 us
    all_to_all x2, blocking collectives, to_columns(): lax.all_to_all(array, 'cols', split_axis=0, concat_axis=0, tiled=True)  36.9 us
    ppermute x17, starting transfers between devices, swap(): return lax.ppermute(array, 'rows', [(i, i ^ k) for i in range(rows)])  35.7 us
    all_to_all x4, waiting for transfers between devices, exchange(): lax.all_to_all(partial, 'cols', split_axis=0, concat_axis=0, tiled=True)  32.1 us
    all_to_all x4, starting transfers between devices, exchange(): lax.all_to_all(partial, 'cols', split_axis=0, concat_axis=0, tiled=True)  19.1 us
    pallas_call x1, Pallas kernels, shards(): pl.pallas_call(functools.partial(lab_kernel, slots, rows), out_shape=shap...  19.1 us
    ppermute x17, waiting for transfers between devices, swap(): return lax.ppermute(array, 'rows', [(i, i ^ k) for i in range(rows)])  16.6 us
    pallas_call x3, Pallas kernels, turn(): pl.pallas_call(functools.partial(pass_kernel, slots), out_shape=shape_of(...  14.8 us
  transfers between devices with their start and end apart: 23, of which 10 were waited for; matrix products, arithmetic and copies ran while one was open for 4% of the time, Pallas kernels for 9%

profile of v2, /device:TPU:1, one launch (start us, length us, event | category | flops | bytes accessed | tf_op | source)
XLA Modules:
  0.0 295.7 jit_solution(8901059613560574776)
XLA Ops:
  7.2 0.0 copy-start
  7.2 0.0 all-gather.2.cloned.1.call-start
  7.2 1.2 slice.36
  8.4 21.7 %all_to_all.58 = bf16[16,96,256]{2,1,0:T(8,128)(2,1)} all-to-all(bf16[16,96,256]{2,1,0:T(8,128)(2,1)S(1)} %slice.36), channel_id=1, replica_groups=mesh['rows'=8,'cols'=16] {'cols'}, dimensions={0} | all-to-all | bytes 1572864 | tf_op jit(solution)/shard_map/all_to_all | solution.py:513
  30.1 0.0 all-gather.2.cloned.1.call-update
  30.2 1.0 slice.37
  31.1 1.4 collective-permute-start
  32.5 2.6 collective-permute-start.1
  35.8 11.3 %prep.1 = (s32[1,128]{1,0:T(1,128)S(1)}, s32[4,128]{1,0:T(4,128)S(1)}, bf16[64,128,128]{2,1,0:T(8,128)(2,1)}, bf16[64,128,128]{2,1,0:T(8,128)(2,1)}, bf16[129,16...) custom-call(s32[1]{0:T(128)} %bitcast.11.row_ref, ...), custom_call_target="tpu_custom_call" | custom-call | flops 1000000000 | bytes 50331648 | tf_op jit(solution)/shard_map/prep/pallas_call | solution.py:518
  47.1 2.6 collective-permute-start.4
  49.8 0.1 pad_maximum_fusion.3
  49.9 15.2 %all_to_all.59.here_any.refs_14_ = bf16[16,4,32,256]{3,2,1,0:T(8,128)(2,1)S(1)} all-to-all(bf16[16,4,32,256]{3,2,1,0:T(8,128)(2,1)S(1)} %pad_maximum_fusion.3), channel_id=1, replica_groups=mesh['rows'=8,'cols'=16] {'cols'}, dimensions={0} | all-to-all | bytes 2097152 | tf_op jit(solution)/shard_map/all_to_all | solution.py:513
  65.1 6.2 %collective-permute-start.3 = (bf16[16,4,32,256]{3,2,1,0:T(8,128)(2,1)S(1)}, bf16[16,4,32,256]{3,2,1,0:T(8,128)(2,1)S(1)}, u32[]{:S(2)}, u32[]{:S(2)}) collective-permute-start(bf16[16,4,32,256]{3,2,1,0:T(8,128)(2,1)S(1)} %all_to_all.59.here_any.refs_14_), channel_id=1, source_target_pairs={{0,16},{16,0},{32,48},{48,32},{64,80},{80,64},{96,112},{112,96},{1... | collective-permute-start | bytes 3145736 | tf_op jit(solution)/shard_map/ppermute | solution.py:510
  71.3 0.8 dynamic-slice_convert_fusion.start_ref
  72.1 0.9 convolution_subtract_fusion.1
  73.0 1.0 convolution_subtract_fusion.side_ref
  74.0 0.2 fusion.4.gram_ref
  74.3 3.2 %all-gather.2.cloned.1.call-done.early_any.refs_13_ = bf16[128,96,256]{2,1,0:T(8,128)(2,1)} async-done(((bf16[16,96,256]{2,1,0:T(8,128)(2,1)}), bf16[128,96,256]{2,1,0:T(8,128)(2,1)}) %all-gather.2.cloned.1.call-update) | async-done | bytes 6291472 | tf_op jit(solution)/shard_map/all_gather | solution.py:544
  77.5 6.8 %first_pass.1 = (f32[8,128,256]{2,1,0:T(8,128)}, bf16[64,128,256]{2,1,0:T(8,128)(2,1)}, bf16[64,256,128]{2,1,0:T(8,128)(2,1)}) custom-call(s32[1]{0:T(128)} %bitcast.11.row_ref, s32[1,128]{1,0:T(1,128)S(1)} %get-tuple-element.291.meta_ref, s32[4,128]{1,0:T(4,128)S(1)} %get-tuple-element.292.work_ref, bf16[64,128,128]{2,1,0:T(8,128)(2,1)} %get-tuple-element.189.xs_any, ...), custom_call_target="tpu_custom_call" | custom-call | tf_op jit(solution)/shard_map/first_pass/pallas_call | solution.py:584
  84.3 5.4 %all-to-all-start.4 = ((f32[16,64,256]{2,1,0:T(8,128)}), f32[16,64,256]{2,1,0:T(8,128)S(1)}, u32[]{:S(2)}, u32[]{:S(2)}) async-start(f32[16,64,256]{2,1,0:T(8,128)} %bitcast.60), calls=%async_computation.4 | async-start | bytes 2097152 | tf_op jit(solution)/shard_map/all_to_all | solution.py:573
  89.7 1.7 fusion.3
  91.4 1.1 pad_maximum_fusion
  92.5 1.1 pad_maximum_fusion.1
  93.6 0.8 collective-permute-start.6
  94.5 1.1 pad_maximum_fusion.2
  95.5 3.0 %collective-permute-start.7 = (bf16[2,129,16,128]{3,2,1,0:T(8,128)(2,1)}, bf16[2,129,16,128]{3,2,1,0:T(8,128)(2,1)}, u32[]{:S(2)}, u32[]{:S(2)}) collective-permute-start(bf16[2,129,16,128]{3,2,1,0:T(8,128)(2,1)} %pad_maximum_fusion.2), channel_id=1, source_target_pairs={{0,96},{16,112},{32,64},{48,80},{64,32},{80,48},{96,0},{112,16},{1... | collective-permute-start | bytes 3170312 | tf_op jit(solution)/shard_map/ppermute | solution.py:510
  98.6 1.1 pad_maximum_fusion.4
  99.6 5.3 %all-to-all-done.4.recv_ref = f32[16,64,256]{2,1,0:T(8,128)S(1)} async-done(((f32[16,64,256]{2,1,0:T(8,128)}), f32[16,64,256]{2,1,0:T(8,128)S(1)}, u32[]{:S(2)}, u32[]{:S(2)}) %all-to-all-start.4) | async-done | bytes 1048608 | tf_op jit(solution)/shard_map/all_to_all | solution.py:573
  104.9 0.3 first_step.1
  105.2 94.0 %while.15 = (s32[]{:T(128)}, f32[4,64,256]{2,1,0:T(8,128)S(1)}, bf16[16,64,256]{2,1,0:T(8,128)(2,1)S(1)}, s32[1,128]{1,0:T(1,128)S(1)}, s32[4,128]{1,0:T(4,128)S...) while((s32[]{:T(128)}, f32[4,64,256]{2,1,0:T(8,128)S(1)}, ...), condition=%wide.region_1.0_spmd, body=%wide.region_0.0_spmd.sunk | while | flops 2 | bytes 3145869 | solution.py:653
  105.3 13.0 %all_to_all.61 = bf16[16,64,256]{2,1,0:T(8,128)(2,1)S(1)} all-to-all(bf16[16,64,256]{2,1,0:T(8,128)(2,1)S(1)} %get-tuple-element.300), channel_id=1, replica_groups=mesh['rows'=8,'cols'=16] {'cols'}, dimensions={0} | all-to-all | bytes 1048576 | tf_op jit(solution)/shard_map/while/body/eval_jaxpr/all_to_all | solution.py:578
  118.3 4.9 %patient_pass.5 = bf16[8,128,256]{2,1,0:T(8,128)(2,1)} custom-call(s32[1,128]{1,0:T(1,128)S(1)} %get-tuple-element.311.meta_ref, s32[4,128]{1,0:T(4,128)S(1)} %get-tuple-element.312.work_ref, bf16[64,128,128]{2,1,0:T(8,128)(2,1)} %get-tuple-element.313.ws_any, bf16[64,128,256]{2,1,0:T(8,128)(2,1)} %get-tuple-element.314.kept_any, ...), custom_call_target="tpu_custom_call" | custom-call | tf_op jit(solution)/shard_map/while/body/eval_jaxpr/patient_pass/pallas_call | solution.py:625
  123.2 4.4 %all-to-all-start.1 = ((bf16[16,64,256]{2,1,0:T(8,128)(2,1)}), bf16[16,64,256]{2,1,0:T(8,128)(2,1)S(1)}, u32[]{:S(2)}, u32[]{:S(2)}) async-start(bf16[16,64,256]{2,1,0:T(8,128)(2,1)} %bitcast.47), calls=%async_computation.1 | async-start | bytes 1048576 | tf_op jit(solution)/shard_map/while/body/eval_jaxpr/all_to_all | solution.py:573
  127.7 8.9 %all-to-all-done.1.recv_ref = bf16[16,64,256]{2,1,0:T(8,128)(2,1)S(1)} async-done(((bf16[16,64,256]{2,1,0:T(8,128)(2,1)}), bf16[16,64,256]{2,1,0:T(8,128)(2,1)S(1)}, u32[]{:S(2)}, u32[]{:S(2)}) %all-to-all-start.1) | async-done | bytes 524320 | tf_op jit(solution)/shard_map/while/body/eval_jaxpr/all_to_all | solution.py:573
  136.6 0.5 step.5
  137.1 12.3 %all_to_all.61 = bf16[16,64,256]{2,1,0:T(8,128)(2,1)S(1)} all-to-all(bf16[16,64,256]{2,1,0:T(8,128)(2,1)S(1)} %get-tuple-element.300), channel_id=1, replica_groups=mesh['rows'=8,'cols'=16] {'cols'}, dimensions={0} | all-to-all | bytes 1048576 | tf_op jit(solution)/shard_map/while/body/eval_jaxpr/all_to_all | solution.py:578
  149.4 4.9 %patient_pass.5 = bf16[8,128,256]{2,1,0:T(8,128)(2,1)} custom-call(s32[1,128]{1,0:T(1,128)S(1)} %get-tuple-element.311.meta_ref, s32[4,128]{1,0:T(4,128)S(1)} %get-tuple-element.312.work_ref, bf16[64,128,128]{2,1,0:T(8,128)(2,1)} %get-tuple-element.313.ws_any, bf16[64,128,256]{2,1,0:T(8,128)(2,1)} %get-tuple-element.314.kept_any, ...), custom_call_target="tpu_custom_call" | custom-call | tf_op jit(solution)/shard_map/while/body/eval_jaxpr/patient_pass/pallas_call | solution.py:625
  154.4 4.7 %all-to-all-start.1 = ((bf16[16,64,256]{2,1,0:T(8,128)(2,1)}), bf16[16,64,256]{2,1,0:T(8,128)(2,1)S(1)}, u32[]{:S(2)}, u32[]{:S(2)}) async-start(bf16[16,64,256]{2,1,0:T(8,128)(2,1)} %bitcast.47), calls=%async_computation.1 | async-start | bytes 1048576 | tf_op jit(solution)/shard_map/while/body/eval_jaxpr/all_to_all | solution.py:573
  159.1 8.9 %all-to-all-done.1.recv_ref = bf16[16,64,256]{2,1,0:T(8,128)(2,1)S(1)} async-done(((bf16[16,64,256]{2,1,0:T(8,128)(2,1)}), bf16[16,64,256]{2,1,0:T(8,128)(2,1)S(1)}, u32[]{:S(2)}, u32[]{:S(2)}) %all-to-all-start.1) | async-done | bytes 524320 | tf_op jit(solution)/shard_map/while/body/eval_jaxpr/all_to_all | solution.py:573
  168.0 0.5 step.5
  168.5 11.9 %all_to_all.61 = bf16[16,64,256]{2,1,0:T(8,128)(2,1)S(1)} all-to-all(bf16[16,64,256]{2,1,0:T(8,128)(2,1)S(1)} %get-tuple-element.300), channel_id=1, replica_groups=mesh['rows'=8,'cols'=16] {'cols'}, dimensions={0} | all-to-all | bytes 1048576 | tf_op jit(solution)/shard_map/while/body/eval_jaxpr/all_to_all | solution.py:578
  180.4 4.9 %patient_pass.5 = bf16[8,128,256]{2,1,0:T(8,128)(2,1)} custom-call(s32[1,128]{1,0:T(1,128)S(1)} %get-tuple-element.311.meta_ref, s32[4,128]{1,0:T(4,128)S(1)} %get-tuple-element.312.work_ref, bf16[64,128,128]{2,1,0:T(8,128)(2,1)} %get-tuple-element.313.ws_any, bf16[64,128,256]{2,1,0:T(8,128)(2,1)} %get-tuple-element.314.kept_any, ...), custom_call_target="tpu_custom_call" | custom-call | tf_op jit(solution)/shard_map/while/body/eval_jaxpr/patient_pass/pallas_call | solution.py:625
  185.4 4.7 %all-to-all-start.1 = ((bf16[16,64,256]{2,1,0:T(8,128)(2,1)}), bf16[16,64,256]{2,1,0:T(8,128)(2,1)S(1)}, u32[]{:S(2)}, u32[]{:S(2)}) async-start(bf16[16,64,256]{2,1,0:T(8,128)(2,1)} %bitcast.47), calls=%async_computation.1 | async-start | bytes 1048576 | tf_op jit(solution)/shard_map/while/body/eval_jaxpr/all_to_all | solution.py:573
  190.1 8.9 %all-to-all-done.1.recv_ref = bf16[16,64,256]{2,1,0:T(8,128)(2,1)S(1)} async-done(((bf16[16,64,256]{2,1,0:T(8,128)(2,1)}), bf16[16,64,256]{2,1,0:T(8,128)(2,1)S(1)}, u32[]{:S(2)}, u32[]{:S(2)}) %all-to-all-start.1) | async-done | bytes 524320 | tf_op jit(solution)/shard_map/while/body/eval_jaxpr/all_to_all | solution.py:573
  199.0 0.2 step.5
  199.2 13.8 %all_to_all.60 = bf16[16,64,256]{2,1,0:T(8,128)(2,1)S(1)} all-to-all(bf16[16,64,256]{2,1,0:T(8,128)(2,1)S(1)} %get-tuple-element.207), channel_id=1, replica_groups=mesh['rows'=8,'cols'=16] {'cols'}, dimensions={0} | all-to-all | bytes 1048576 | tf_op jit(solution)/shard_map/all_to_all | solution.py:578
  213.0 1.2 collective-permute-start.8
  214.2 8.4 %collective-permute-done.9.refs_5_ = bf16[8,128,256]{2,1,0:T(8,128)(2,1)S(1)} collective-permute-done((bf16[8,128,256]{2,1,0:T(8,128)(2,1)S(1)}, bf16[8,128,256]{2,1,0:T(8,128)(2,1)S(1)}, u32[]{:S(2)}, u32[]{:S(2)}) %collective-permute-start.9) | collective-permute-done | bytes 524320 | tf_op jit(solution)/shard_map/ppermute | solution.py:510
  222.6 14.4 %collective-permute-start.12 = (bf16[8,128,256]{2,1,0:T(8,128)(2,1)S(1)}, bf16[8,128,256]{2,1,0:T(8,128)(2,1)S(1)}, u32[]{:S(2)}, u32[]{:S(2)}) collective-permute-start(bf16[8,128,256]{2,1,0:T(8,128)(2,1)S(1)} %bitcast.51), channel_id=1, source_target_pairs={{0,16},{16,0},{32,48},{48,32},{64,80},{80,64},{96,112},{112,96},{1... | collective-permute-start | bytes 1572872 | tf_op jit(solution)/shard_map/ppermute | solution.py:510
  237.0 0.1 collective-permute-start.10
  237.1 0.1 collective-permute-start.13
  237.2 0.5 collective-permute-start.14
  237.7 1.2 collective-permute-start.11
  238.9 6.1 %collective-permute-done.10.refs_6_ = bf16[4,128,256]{2,1,0:T(8,128)(2,1)S(1)} collective-permute-done((bf16[4,128,256]{2,1,0:T(8,128)(2,1)S(1)}, bf16[4,128,256]{2,1,0:T(8,128)(2,1)S(1)}, u32[]{:S(2)}, u32[]{:S(2)}) %collective-permute-start.10) | collective-permute-done | bytes 262176 | tf_op jit(solution)/shard_map/ppermute | solution.py:510
  245.0 0.8 collective-permute-start.15
  245.8 1.0 collective-permute-done.11.refs_7_
  246.8 0.9 collective-permute-start.16
  247.7 1.1 collective-permute-done.16.refs_12_
  248.8 19.1 %lab_step.1 = bf16[128,16,256]{2,1,0:T(8,128)(2,1)} custom-call(s32[1]{0:T(128)} %bitcast.11.row_ref, bf16[129,16,128]{2,1,0:T(8,128)(2,1)S(1)} %copy-done.5, bf16[4,129,16,128]{3,2,1,0:T(8,128)(2,1)} %collective-permute-done.4.other_any, bf16[2,129,16,128]{3,2,1,0:T(8,128)(2,1)} %collective-permute-done.5.refs_0_, ...), custom_call_target="tpu_custom_call" | custom-call | tf_op jit(solution)/shard_map/lab_step/pallas_call | solution.py:662
  267.9 4.0 %all-to-all-start.6 = ((bf16[8,256,256]{2,1,0:T(8,128)(2,1)}), bf16[8,256,256]{2,1,0:T(8,128)(2,1)S(1)}, u32[]{:S(2)}, u32[]{:S(2)}) async-start(bf16[8,256,256]{2,1,0:T(8,128)(2,1)} %bitcast.23), calls=%async_computation.6 | async-start | bytes 2097152 | tf_op jit(solution)/shard_map/all_to_all | solution.py:686
  271.9 0.6 slice_bitcast_fusion.1
  272.5 14.5 %all-to-all-done.6 = bf16[8,256,256]{2,1,0:T(8,128)(2,1)S(1)} async-done(((bf16[8,256,256]{2,1,0:T(8,128)(2,1)}), bf16[8,256,256]{2,1,0:T(8,128)(2,1)S(1)}, u32[]{:S(2)}, u32[]{:S(2)}) %all-to-all-start.6) | async-done | bytes 1048608 | tf_op jit(solution)/shard_map/all_to_all | solution.py:686
  287.0 0.3 fusion
  287.3 1.5 copy.27
  (43 shorter events, 0.2 us)
Async XLA Ops:
  7.2 64.9 %copy-start = (bf16[256,256]{1,0:T(8,128)(2,1)S(1)}, bf16[256,256]{1,0:T(8,128)(2,1)}, u32[]{:S(2)}) copy-start(bf16[256,256]{1,0:T(8,128)(2,1)} %param.19) | copy-start | bytes 393220
  7.2 70.3 %all-gather.2.cloned.1.call-start = ((), (), s32[]{:S(2)}) async-start(), calls=%async_computation.7 | async-start | bytes 7077888 | tf_op jit(solution)/shard_map/all_gather | solution.py:544
  31.1 18.6 %collective-permute-start = (bf16[16,32,256]{2,1,0:T(8,128)(2,1)S(1)}, bf16[16,32,256]{2,1,0:T(8,128)(2,1)S(1)}, u32[]{:S(2)}, u32[]{:S(2)}) collective-permute-start(bf16[16,32,256]{2,1,0:T(8,128)(2,1)S(1)} %slice.37), channel_id=1, source_target_pairs={{0,32},{16,48},{32,0},{48,16},{64,96},{80,112},{96,64},{112,80},{1... | collective-permute-start | bytes 786440 | tf_op jit(solution)/shard_map/ppermute | solution.py:510
  32.5 17.2 %collective-permute-start.1 = (bf16[16,32,256]{2,1,0:T(8,128)(2,1)S(1)}, bf16[16,32,256]{2,1,0:T(8,128)(2,1)S(1)}, u32[]{:S(2)}, u32[]{:S(2)}) collective-permute-start(bf16[16,32,256]{2,1,0:T(8,128)(2,1)S(1)} %slice.37), channel_id=1, source_target_pairs={{0,64},{16,80},{32,96},{48,112},{64,0},{80,16},{96,32},{112,48},{1... | collective-permute-start | bytes 786440 | tf_op jit(solution)/shard_map/ppermute | solution.py:510
  35.1 14.6 %collective-permute-start.2 = (bf16[16,32,256]{2,1,0:T(8,128)(2,1)S(1)}, bf16[16,32,256]{2,1,0:T(8,128)(2,1)S(1)}, u32[]{:S(2)}, u32[]{:S(2)}) collective-permute-start(bf16[16,32,256]{2,1,0:T(8,128)(2,1)S(1)} %slice.37), channel_id=1, source_target_pairs={{0,96},{16,112},{32,64},{48,80},{64,32},{80,48},{96,0},{112,16},{1... | collective-permute-start | bytes 786440 | tf_op jit(solution)/shard_map/ppermute | solution.py:510
  47.1 27.1 %collective-permute-start.4 = (bf16[4,129,16,128]{3,2,1,0:T(8,128)(2,1)}, bf16[4,129,16,128]{3,2,1,0:T(8,128)(2,1)}, u32[]{:S(2)}, u32[]{:S(2)}) collective-permute-start(bf16[4,129,16,128]{3,2,1,0:T(8,128)(2,1)} %get-tuple-element.185), channel_id=1, source_target_pairs={{0,16},{16,0},{32,48},{48,32},{64,80},{80,64},{96,112},{112,96},{1... | collective-permute-start | bytes 6340616 | tf_op jit(solution)/shard_map/ppermute | solution.py:510
  65.1 12.3 %copy-start.1 = (bf16[16,4,32,256]{3,2,1,0:T(8,128)(2,1)}, bf16[16,4,32,256]{3,2,1,0:T(8,128)(2,1)S(1)}, u32[]{:S(2)}) copy-start(bf16[16,4,32,256]{3,2,1,0:T(8,128)(2,1)S(1)} %all_to_all.59.here_any.refs_14_) | copy-start | bytes 3145732
  65.1 9.1 %collective-permute-start.3 = (bf16[16,4,32,256]{3,2,1,0:T(8,128)(2,1)S(1)}, bf16[16,4,32,256]{3,2,1,0:T(8,128)(2,1)S(1)}, u32[]{:S(2)}, u32[]{:S(2)}) collective-permute-start(bf16[16,4,32,256]{3,2,1,0:T(8,128)(2,1)S(1)} %all_to_all.59.here_any.refs_14_), channel_id=1, source_target_pairs={{0,16},{16,0},{32,48},{48,32},{64,80},{80,64},{96,112},{112,96},{1... | collective-permute-start | bytes 3145736 | tf_op jit(solution)/shard_map/ppermute | solution.py:510
  74.2 3.2 %copy-start.3 = (bf16[16,4,32,256]{3,2,1,0:T(8,128)(2,1)}, bf16[16,4,32,256]{3,2,1,0:T(8,128)(2,1)S(1)}, u32[]{:S(2)}) copy-start(bf16[16,4,32,256]{3,2,1,0:T(8,128)(2,1)S(1)} %collective-permute-done.3.there_any.refs_15_) | copy-start | bytes 3145732
  84.3 20.6 %all-to-all-start.4 = ((f32[16,64,256]{2,1,0:T(8,128)}), f32[16,64,256]{2,1,0:T(8,128)S(1)}, u32[]{:S(2)}, u32[]{:S(2)}) async-start(f32[16,64,256]{2,1,0:T(8,128)} %bitcast.60), calls=%async_computation.4 | async-start | bytes 2097152 | tf_op jit(solution)/shard_map/all_to_all | solution.py:573
  89.7 1.7 copy-start.10
  89.7 2.8 copy-start.9
  91.4 3.0 %copy-start.8 = (bf16[129,16,128]{2,1,0:T(8,128)(2,1)S(1)}, bf16[129,16,128]{2,1,0:T(8,128)(2,1)}, u32[]{:S(2)}) copy-start(bf16[129,16,128]{2,1,0:T(8,128)(2,1)} %get-tuple-element.206) | copy-start | bytes 1585156
  92.5 144.6 %collective-permute-start.5 = (bf16[2,129,16,128]{3,2,1,0:T(8,128)(2,1)}, bf16[2,129,16,128]{3,2,1,0:T(8,128)(2,1)}, u32[]{:S(2)}, u32[]{:S(2)}) collective-permute-start(bf16[2,129,16,128]{3,2,1,0:T(8,128)(2,1)} %pad_maximum_fusion), channel_id=1, source_target_pairs={{0,32},{16,48},{32,0},{48,16},{64,96},{80,112},{96,64},{112,80},{1... | collective-permute-start | bytes 3170312 | tf_op jit(solution)/shard_map/ppermute | solution.py:510
  92.5 6.0 %copy-start.2 = (bf16[16,4,32,256]{3,2,1,0:T(8,128)(2,1)S(1)}, bf16[16,4,32,256]{3,2,1,0:T(8,128)(2,1)}, u32[]{:S(2)}) copy-start(bf16[16,4,32,256]{3,2,1,0:T(8,128)(2,1)} %copy-done.1) | copy-start | bytes 3145732
  92.5 6.0 %copy-start.6 = (bf16[16,96,256]{2,1,0:T(8,128)(2,1)S(1)}, bf16[16,96,256]{2,1,0:T(8,128)(2,1)}, u32[]{:S(2)}) copy-start(bf16[16,96,256]{2,1,0:T(8,128)(2,1)} %all_to_all.58) | copy-start | bytes 2359300
  93.6 143.6 %collective-permute-start.6 = (bf16[2,129,16,128]{3,2,1,0:T(8,128)(2,1)}, bf16[2,129,16,128]{3,2,1,0:T(8,128)(2,1)}, u32[]{:S(2)}, u32[]{:S(2)}) collective-permute-start(bf16[2,129,16,128]{3,2,1,0:T(8,128)(2,1)} %pad_maximum_fusion.1), channel_id=1, source_target_pairs={{0,64},{16,80},{32,96},{48,112},{64,0},{80,16},{96,32},{112,48},{1... | collective-permute-start | bytes 3170312 | tf_op jit(solution)/shard_map/ppermute | solution.py:510
  95.5 142.2 %collective-permute-start.7 = (bf16[2,129,16,128]{3,2,1,0:T(8,128)(2,1)}, bf16[2,129,16,128]{3,2,1,0:T(8,128)(2,1)}, u32[]{:S(2)}, u32[]{:S(2)}) collective-permute-start(bf16[2,129,16,128]{3,2,1,0:T(8,128)(2,1)} %pad_maximum_fusion.2), channel_id=1, source_target_pairs={{0,96},{16,112},{32,64},{48,80},{64,32},{80,48},{96,0},{112,16},{1... | collective-permute-start | bytes 3170312 | tf_op jit(solution)/shard_map/ppermute | solution.py:510
  123.2 13.4 %all-to-all-start.1 = ((bf16[16,64,256]{2,1,0:T(8,128)(2,1)}), bf16[16,64,256]{2,1,0:T(8,128)(2,1)S(1)}, u32[]{:S(2)}, u32[]{:S(2)}) async-start(bf16[16,64,256]{2,1,0:T(8,128)(2,1)} %bitcast.47), calls=%async_computation.1 | async-start | bytes 1048576 | tf_op jit(solution)/shard_map/while/body/eval_jaxpr/all_to_all | solution.py:573
  154.4 13.6 %all-to-all-start.1 = ((bf16[16,64,256]{2,1,0:T(8,128)(2,1)}), bf16[16,64,256]{2,1,0:T(8,128)(2,1)S(1)}, u32[]{:S(2)}, u32[]{:S(2)}) async-start(bf16[16,64,256]{2,1,0:T(8,128)(2,1)} %bitcast.47), calls=%async_computation.1 | async-start | bytes 1048576 | tf_op jit(solution)/shard_map/while/body/eval_jaxpr/all_to_all | solution.py:573
  185.4 13.6 %all-to-all-start.1 = ((bf16[16,64,256]{2,1,0:T(8,128)(2,1)}), bf16[16,64,256]{2,1,0:T(8,128)(2,1)S(1)}, u32[]{:S(2)}, u32[]{:S(2)}) async-start(bf16[16,64,256]{2,1,0:T(8,128)(2,1)} %bitcast.47), calls=%async_computation.1 | async-start | bytes 1048576 | tf_op jit(solution)/shard_map/while/body/eval_jaxpr/all_to_all | solution.py:573
  199.2 49.6 %copy-start.4 = (bf16[16,4,32,256]{3,2,1,0:T(8,128)(2,1)S(1)}, bf16[16,4,32,256]{3,2,1,0:T(8,128)(2,1)}, u32[]{:S(2)}) copy-start(bf16[16,4,32,256]{3,2,1,0:T(8,128)(2,1)} %copy-done.3) | copy-start | bytes 3145732
  199.2 49.6 %copy-start.5 = (bf16[129,16,128]{2,1,0:T(8,128)(2,1)S(1)}, bf16[129,16,128]{2,1,0:T(8,128)(2,1)}, u32[]{:S(2)}) copy-start(bf16[129,16,128]{2,1,0:T(8,128)(2,1)} %get-tuple-element.202.same_any) | copy-start | bytes 1585156
  213.0 9.5 %collective-permute-start.9 = (bf16[8,128,256]{2,1,0:T(8,128)(2,1)S(1)}, bf16[8,128,256]{2,1,0:T(8,128)(2,1)S(1)}, u32[]{:S(2)}, u32[]{:S(2)}) collective-permute-start(bf16[8,128,256]{2,1,0:T(8,128)(2,1)S(1)} %bitcast.49), channel_id=1, source_target_pairs={{0,96},{16,112},{32,64},{48,80},{64,32},{80,48},{96,0},{112,16},{1... | collective-permute-start | bytes 1572872 | tf_op jit(solution)/shard_map/ppermute | solution.py:510
  213.0 23.9 %collective-permute-start.8 = (bf16[8,128,256]{2,1,0:T(8,128)(2,1)S(1)}, bf16[8,128,256]{2,1,0:T(8,128)(2,1)S(1)}, u32[]{:S(2)}, u32[]{:S(2)}) collective-permute-start(bf16[8,128,256]{2,1,0:T(8,128)(2,1)S(1)} %bitcast.50), channel_id=1, source_target_pairs={{0,32},{16,48},{32,0},{48,16},{64,96},{80,112},{96,64},{112,80},{1... | collective-permute-start | bytes 1572872 | tf_op jit(solution)/shard_map/ppermute | solution.py:510
  222.6 25.1 %collective-permute-start.12 = (bf16[8,128,256]{2,1,0:T(8,128)(2,1)S(1)}, bf16[8,128,256]{2,1,0:T(8,128)(2,1)S(1)}, u32[]{:S(2)}, u32[]{:S(2)}) collective-permute-start(bf16[8,128,256]{2,1,0:T(8,128)(2,1)S(1)} %bitcast.51), channel_id=1, source_target_pairs={{0,16},{16,0},{32,48},{48,32},{64,80},{80,64},{96,112},{112,96},{1... | collective-permute-start | bytes 1572872 | tf_op jit(solution)/shard_map/ppermute | solution.py:510
  237.0 8.0 %collective-permute-start.10 = (bf16[4,128,256]{2,1,0:T(8,128)(2,1)S(1)}, bf16[4,128,256]{2,1,0:T(8,128)(2,1)S(1)}, u32[]{:S(2)}, u32[]{:S(2)}) collective-permute-start(bf16[4,128,256]{2,1,0:T(8,128)(2,1)S(1)} %slice.38), channel_id=1, source_target_pairs={{0,32},{16,48},{32,0},{48,16},{64,96},{80,112},{96,64},{112,80},{1... | collective-permute-start | bytes 786440 | tf_op jit(solution)/shard_map/ppermute | solution.py:510
  237.1 10.6 %collective-permute-start.13 = (bf16[8,128,256]{2,1,0:T(8,128)(2,1)S(1)}, bf16[8,128,256]{2,1,0:T(8,128)(2,1)S(1)}, u32[]{:S(2)}, u32[]{:S(2)}) collective-permute-start(bf16[8,128,256]{2,1,0:T(8,128)(2,1)S(1)} %collective-permute-done.8.refs_4_), channel_id=1, source_target_pairs={{0,16},{16,0},{32,48},{48,32},{64,80},{80,64},{96,112},{112,96},{1... | collective-permute-start | bytes 1572872 | tf_op jit(solution)/shard_map/ppermute | solution.py:510
  237.2 10.5 %collective-permute-start.14 = (bf16[8,128,256]{2,1,0:T(8,128)(2,1)S(1)}, bf16[8,128,256]{2,1,0:T(8,128)(2,1)S(1)}, u32[]{:S(2)}, u32[]{:S(2)}) collective-permute-start(bf16[8,128,256]{2,1,0:T(8,128)(2,1)S(1)} %collective-permute-done.9.refs_5_), channel_id=1, source_target_pairs={{0,16},{16,0},{32,48},{48,32},{64,80},{80,64},{96,112},{112,96},{1... | collective-permute-start | bytes 1572872 | tf_op jit(solution)/shard_map/ppermute | solution.py:510
  237.7 9.1 %collective-permute-start.11 = (bf16[4,128,256]{2,1,0:T(8,128)(2,1)S(1)}, bf16[4,128,256]{2,1,0:T(8,128)(2,1)S(1)}, u32[]{:S(2)}, u32[]{:S(2)}) collective-permute-start(bf16[4,128,256]{2,1,0:T(8,128)(2,1)S(1)} %slice.39), channel_id=1, source_target_pairs={{0,96},{16,112},{32,64},{48,80},{64,32},{80,48},{96,0},{112,16},{1... | collective-permute-start | bytes 786440 | tf_op jit(solution)/shard_map/ppermute | solution.py:510
  245.0 2.7 collective-permute-start.15
  246.8 2.0 collective-permute-start.16
  267.9 19.1 %copy-start.7 = (bf16[16,128,256]{2,1,0:T(8,128)(2,1)S(1)}, bf16[16,128,256]{2,1,0:T(8,128)(2,1)}, u32[]{:S(2)}) copy-start(bf16[16,128,256]{2,1,0:T(8,128)(2,1)} %pad_maximum_fusion.4) | copy-start | bytes 3145732
  267.9 19.1 %all-to-all-start.6 = ((bf16[8,256,256]{2,1,0:T(8,128)(2,1)}), bf16[8,256,256]{2,1,0:T(8,128)(2,1)S(1)}, u32[]{:S(2)}, u32[]{:S(2)}) async-start(bf16[8,256,256]{2,1,0:T(8,128)(2,1)} %bitcast.23), calls=%async_computation.6 | async-start | bytes 2097152 | tf_op jit(solution)/shard_map/all_to_all | solution.py:686
Sparse Core Ops, SparseCore 0:
  30.3 47.1 all-gather.1

commit v3 on v2

--- a/solution.py
+++ b/solution.py
@@ -680,7 +680,7 @@
             pltpu.SemaphoreType.DMA((rows,)),
             pltpu.SemaphoreType.DMA,
         ],
-        compiler_params=params(44),
+        compiler_params=params(36),
         name="lab_step",
     )(row, same[0], other, *pieces, *factors, labs, late_here, late_there)
     back = lax.all_to_all(

time: 295 us -> 295 us (level)
  transfers between devices with their start and end apart: 23 -> 23, of which waited for: 10 -> 10; matrix products, arithmetic and copies ran while one was open for 4% -> 4% of each run, Pallas kernels for 9% -> 10%
where the time goes in v3:
time: 295 us
  blocking collectives  87.4 us (30%)
  waiting for transfers between devices  67.3 us (23%)
  starting transfers between devices  56.3 us (19%)
  Pallas kernels  54.6 us (19%)
  between operations  15 us (5%)
  local copies, waits for them, and re-layouts  6.21 us (2%)
  other arithmetic  5.48 us (2%)
    all_to_all x4, blocking collectives, to_all(): lax.all_to_all(probe, 'cols', split_axis=0, concat_axis=0, tiled=True)  50.4 us
    all_to_all x2, blocking collectives, to_columns(): lax.all_to_all(array, 'cols', split_axis=0, concat_axis=0, tiled=True)  36.9 us
    ppermute x17, starting transfers between devices, swap(): return lax.ppermute(array, 'rows', [(i, i ^ k) for i in range(rows)])  34.5 us
    all_to_all x4, waiting for transfers between devices, exchange(): lax.all_to_all(partial, 'cols', split_axis=0, concat_axis=0, tiled=True)  32.3 us
    pallas_call x1, Pallas kernels, shards(): pl.pallas_call(functools.partial(lab_kernel, slots, rows), out_shape=shap...  17.9 us
    all_to_all x4, starting transfers between devices, exchange(): lax.all_to_all(partial, 'cols', split_axis=0, concat_axis=0, tiled=True)  17.8 us
    ppermute x17, waiting for transfers between devices, swap(): return lax.ppermute(array, 'rows', [(i, i ^ k) for i in range(rows)])  17.3 us
    pallas_call x3, Pallas kernels, turn(): pl.pallas_call(functools.partial(pass_kernel, slots), out_shape=shape_of(...  16 us
  transfers between devices with their start and end apart: 23, of which 10 were waited for; matrix products, arithmetic and copies ran while one was open for 4% of the time, Pallas kernels for 10%

profile of v3, /device:TPU:1, one launch (start us, length us, event | category | flops | bytes accessed | tf_op | source)
XLA Modules:
  0.0 294.5 jit_solution(13041600951401618716)
XLA Ops:
  7.2 0.0 copy-start
  7.2 0.0 all-gather.2.cloned.1.call-start
  7.2 1.2 slice.36
  8.4 21.7 %all_to_all.58 = bf16[16,96,256]{2,1,0:T(8,128)(2,1)} all-to-all(bf16[16,96,256]{2,1,0:T(8,128)(2,1)S(1)} %slice.36), channel_id=1, replica_groups=mesh['rows'=8,'cols'=16] {'cols'}, dimensions={0} | all-to-all | bytes 1572864 | tf_op jit(solution)/shard_map/all_to_all | solution.py:513
  30.1 0.0 all-gather.2.cloned.1.call-update
  30.2 1.0 slice.37
  31.1 1.4 collective-permute-start
  32.5 2.6 collective-permute-start.1
  35.1 0.0 collective-permute-start.2
  35.8 11.3 %prep.1 = (s32[1,128]{1,0:T(1,128)S(1)}, s32[4,128]{1,0:T(4,128)S(1)}, bf16[64,128,128]{2,1,0:T(8,128)(2,1)}, bf16[64,128,128]{2,1,0:T(8,128)(2,1)}, bf16[129,16...) custom-call(s32[1]{0:T(128)} %bitcast.11.row_ref, ...), custom_call_target="tpu_custom_call" | custom-call | flops 1000000000 | bytes 50331648 | tf_op jit(solution)/shard_map/prep/pallas_call | solution.py:518
  47.1 2.6 collective-permute-start.4
  49.8 0.1 pad_maximum_fusion.3
  49.9 15.2 %all_to_all.59.here_any.refs_14_ = bf16[16,4,32,256]{3,2,1,0:T(8,128)(2,1)S(1)} all-to-all(bf16[16,4,32,256]{3,2,1,0:T(8,128)(2,1)S(1)} %pad_maximum_fusion.3), channel_id=1, replica_groups=mesh['rows'=8,'cols'=16] {'cols'}, dimensions={0} | all-to-all | bytes 2097152 | tf_op jit(solution)/shard_map/all_to_all | solution.py:513
  65.1 6.2 %collective-permute-start.3 = (bf16[16,4,32,256]{3,2,1,0:T(8,128)(2,1)S(1)}, bf16[16,4,32,256]{3,2,1,0:T(8,128)(2,1)S(1)}, u32[]{:S(2)}, u32[]{:S(2)}) collective-permute-start(bf16[16,4,32,256]{3,2,1,0:T(8,128)(2,1)S(1)} %all_to_all.59.here_any.refs_14_), channel_id=1, source_target_pairs={{0,16},{16,0},{32,48},{48,32},{64,80},{80,64},{96,112},{112,96},{1... | collective-permute-start | bytes 3145736 | tf_op jit(solution)/shard_map/ppermute | solution.py:510
  71.3 0.8 dynamic-slice_convert_fusion.start_ref
  72.1 0.9 convolution_subtract_fusion.1
  73.0 1.0 convolution_subtract_fusion.side_ref
  74.0 0.2 fusion.4.gram_ref
  74.3 3.2 %all-gather.2.cloned.1.call-done.early_any.refs_13_ = bf16[128,96,256]{2,1,0:T(8,128)(2,1)} async-done(((bf16[16,96,256]{2,1,0:T(8,128)(2,1)}), bf16[128,96,256]{2,1,0:T(8,128)(2,1)}) %all-gather.2.cloned.1.call-update) | async-done | bytes 6291472 | tf_op jit(solution)/shard_map/all_gather | solution.py:544
  77.5 7.9 %first_pass.1 = (f32[8,128,256]{2,1,0:T(8,128)}, bf16[64,128,256]{2,1,0:T(8,128)(2,1)}, bf16[64,256,128]{2,1,0:T(8,128)(2,1)}) custom-call(s32[1]{0:T(128)} %bitcast.11.row_ref, s32[1,128]{1,0:T(1,128)S(1)} %get-tuple-element.291.meta_ref, s32[4,128]{1,0:T(4,128)S(1)} %get-tuple-element.292.work_ref, bf16[64,128,128]{2,1,0:T(8,128)(2,1)} %get-tuple-element.189.xs_any, ...), custom_call_target="tpu_custom_call" | custom-call | tf_op jit(solution)/shard_map/first_pass/pallas_call | solution.py:584
  85.3 4.7 %all-to-all-start.4 = ((f32[16,64,256]{2,1,0:T(8,128)}), f32[16,64,256]{2,1,0:T(8,128)S(1)}, u32[]{:S(2)}, u32[]{:S(2)}) async-start(f32[16,64,256]{2,1,0:T(8,128)} %bitcast.60), calls=%async_computation.4 | async-start | bytes 2097152 | tf_op jit(solution)/shard_map/all_to_all | solution.py:573
  90.0 1.7 fusion.3
  91.8 1.1 pad_maximum_fusion
  92.8 1.1 pad_maximum_fusion.1
  93.9 1.1 pad_maximum_fusion.2
  95.0 3.8 %collective-permute-start.7 = (bf16[2,129,16,128]{3,2,1,0:T(8,128)(2,1)}, bf16[2,129,16,128]{3,2,1,0:T(8,128)(2,1)}, u32[]{:S(2)}, u32[]{:S(2)}) collective-permute-start(bf16[2,129,16,128]{3,2,1,0:T(8,128)(2,1)} %pad_maximum_fusion.2), channel_id=1, source_target_pairs={{0,96},{16,112},{32,64},{48,80},{64,32},{80,48},{96,0},{112,16},{1... | collective-permute-start | bytes 3170312 | tf_op jit(solution)/shard_map/ppermute | solution.py:510
  98.9 1.1 pad_maximum_fusion.4
  99.9 5.5 %all-to-all-done.4.recv_ref = f32[16,64,256]{2,1,0:T(8,128)S(1)} async-done(((f32[16,64,256]{2,1,0:T(8,128)}), f32[16,64,256]{2,1,0:T(8,128)S(1)}, u32[]{:S(2)}, u32[]{:S(2)}) %all-to-all-start.4) | async-done | bytes 1048608 | tf_op jit(solution)/shard_map/all_to_all | solution.py:573
  105.4 0.3 first_step.1
  105.8 94.6 %while.15 = (s32[]{:T(128)}, f32[4,64,256]{2,1,0:T(8,128)S(1)}, bf16[16,64,256]{2,1,0:T(8,128)(2,1)S(1)}, s32[1,128]{1,0:T(1,128)S(1)}, s32[4,128]{1,0:T(4,128)S...) while((s32[]{:T(128)}, f32[4,64,256]{2,1,0:T(8,128)S(1)}, ...), condition=%wide.region_1.0_spmd, body=%wide.region_0.0_spmd.sunk | while | flops 2 | bytes 3145869 | solution.py:653
  105.8 13.1 %all_to_all.61 = bf16[16,64,256]{2,1,0:T(8,128)(2,1)S(1)} all-to-all(bf16[16,64,256]{2,1,0:T(8,128)(2,1)S(1)} %get-tuple-element.300), channel_id=1, replica_groups=mesh['rows'=8,'cols'=16] {'cols'}, dimensions={0} | all-to-all | bytes 1048576 | tf_op jit(solution)/shard_map/while/body/eval_jaxpr/all_to_all | solution.py:578
  118.9 5.3 %patient_pass.5 = bf16[8,128,256]{2,1,0:T(8,128)(2,1)} custom-call(s32[1,128]{1,0:T(1,128)S(1)} %get-tuple-element.311.meta_ref, s32[4,128]{1,0:T(4,128)S(1)} %get-tuple-element.312.work_ref, bf16[64,128,128]{2,1,0:T(8,128)(2,1)} %get-tuple-element.313.ws_any, bf16[64,128,256]{2,1,0:T(8,128)(2,1)} %get-tuple-element.314.kept_any, ...), custom_call_target="tpu_custom_call" | custom-call | tf_op jit(solution)/shard_map/while/body/eval_jaxpr/patient_pass/pallas_call | solution.py:625
  124.2 4.4 %all-to-all-start.1 = ((bf16[16,64,256]{2,1,0:T(8,128)(2,1)}), bf16[16,64,256]{2,1,0:T(8,128)(2,1)S(1)}, u32[]{:S(2)}, u32[]{:S(2)}) async-start(bf16[16,64,256]{2,1,0:T(8,128)(2,1)} %bitcast.47), calls=%async_computation.1 | async-start | bytes 1048576 | tf_op jit(solution)/shard_map/while/body/eval_jaxpr/all_to_all | solution.py:573
  128.7 8.9 %all-to-all-done.1.recv_ref = bf16[16,64,256]{2,1,0:T(8,128)(2,1)S(1)} async-done(((bf16[16,64,256]{2,1,0:T(8,128)(2,1)}), bf16[16,64,256]{2,1,0:T(8,128)(2,1)S(1)}, u32[]{:S(2)}, u32[]{:S(2)}) %all-to-all-start.1) | async-done | bytes 524320 | tf_op jit(solution)/shard_map/while/body/eval_jaxpr/all_to_all | solution.py:573
  137.6 0.5 step.5
  138.1 12.3 %all_to_all.61 = bf16[16,64,256]{2,1,0:T(8,128)(2,1)S(1)} all-to-all(bf16[16,64,256]{2,1,0:T(8,128)(2,1)S(1)} %get-tuple-element.300), channel_id=1, replica_groups=mesh['rows'=8,'cols'=16] {'cols'}, dimensions={0} | all-to-all | bytes 1048576 | tf_op jit(solution)/shard_map/while/body/eval_jaxpr/all_to_all | solution.py:578
  150.4 5.3 %patient_pass.5 = bf16[8,128,256]{2,1,0:T(8,128)(2,1)} custom-call(s32[1,128]{1,0:T(1,128)S(1)} %get-tuple-element.311.meta_ref, s32[4,128]{1,0:T(4,128)S(1)} %get-tuple-element.312.work_ref, bf16[64,128,128]{2,1,0:T(8,128)(2,1)} %get-tuple-element.313.ws_any, bf16[64,128,256]{2,1,0:T(8,128)(2,1)} %get-tuple-element.314.kept_any, ...), custom_call_target="tpu_custom_call" | custom-call | tf_op jit(solution)/shard_map/while/body/eval_jaxpr/patient_pass/pallas_call | solution.py:625
  155.8 4.3 %all-to-all-start.1 = ((bf16[16,64,256]{2,1,0:T(8,128)(2,1)}), bf16[16,64,256]{2,1,0:T(8,128)(2,1)S(1)}, u32[]{:S(2)}, u32[]{:S(2)}) async-start(bf16[16,64,256]{2,1,0:T(8,128)(2,1)} %bitcast.47), calls=%async_computation.1 | async-start | bytes 1048576 | tf_op jit(solution)/shard_map/while/body/eval_jaxpr/all_to_all | solution.py:573
  160.2 8.9 %all-to-all-done.1.recv_ref = bf16[16,64,256]{2,1,0:T(8,128)(2,1)S(1)} async-done(((bf16[16,64,256]{2,1,0:T(8,128)(2,1)}), bf16[16,64,256]{2,1,0:T(8,128)(2,1)S(1)}, u32[]{:S(2)}, u32[]{:S(2)}) %all-to-all-start.1) | async-done | bytes 524320 | tf_op jit(solution)/shard_map/while/body/eval_jaxpr/all_to_all | solution.py:573
  169.1 0.5 step.5
  169.6 11.9 %all_to_all.61 = bf16[16,64,256]{2,1,0:T(8,128)(2,1)S(1)} all-to-all(bf16[16,64,256]{2,1,0:T(8,128)(2,1)S(1)} %get-tuple-element.300), channel_id=1, replica_groups=mesh['rows'=8,'cols'=16] {'cols'}, dimensions={0} | all-to-all | bytes 1048576 | tf_op jit(solution)/shard_map/while/body/eval_jaxpr/all_to_all | solution.py:578
  181.5 5.3 %patient_pass.5 = bf16[8,128,256]{2,1,0:T(8,128)(2,1)} custom-call(s32[1,128]{1,0:T(1,128)S(1)} %get-tuple-element.311.meta_ref, s32[4,128]{1,0:T(4,128)S(1)} %get-tuple-element.312.work_ref, bf16[64,128,128]{2,1,0:T(8,128)(2,1)} %get-tuple-element.313.ws_any, bf16[64,128,256]{2,1,0:T(8,128)(2,1)} %get-tuple-element.314.kept_any, ...), custom_call_target="tpu_custom_call" | custom-call | tf_op jit(solution)/shard_map/while/body/eval_jaxpr/patient_pass/pallas_call | solution.py:625
  186.9 4.3 %all-to-all-start.1 = ((bf16[16,64,256]{2,1,0:T(8,128)(2,1)}), bf16[16,64,256]{2,1,0:T(8,128)(2,1)S(1)}, u32[]{:S(2)}, u32[]{:S(2)}) async-start(bf16[16,64,256]{2,1,0:T(8,128)(2,1)} %bitcast.47), calls=%async_computation.1 | async-start | bytes 1048576 | tf_op jit(solution)/shard_map/while/body/eval_jaxpr/all_to_all | solution.py:573
  191.3 8.9 %all-to-all-done.1.recv_ref = bf16[16,64,256]{2,1,0:T(8,128)(2,1)S(1)} async-done(((bf16[16,64,256]{2,1,0:T(8,128)(2,1)}), bf16[16,64,256]{2,1,0:T(8,128)(2,1)S(1)}, u32[]{:S(2)}, u32[]{:S(2)}) %all-to-all-start.1) | async-done | bytes 524320 | tf_op jit(solution)/shard_map/while/body/eval_jaxpr/all_to_all | solution.py:573
  200.2 0.2 step.5
  200.4 13.1 %all_to_all.60 = bf16[16,64,256]{2,1,0:T(8,128)(2,1)S(1)} all-to-all(bf16[16,64,256]{2,1,0:T(8,128)(2,1)S(1)} %get-tuple-element.207), channel_id=1, replica_groups=mesh['rows'=8,'cols'=16] {'cols'}, dimensions={0} | all-to-all | bytes 1048576 | tf_op jit(solution)/shard_map/all_to_all | solution.py:578
  213.6 0.5 collective-permute-start.8
  214.1 9.1 %collective-permute-done.9.refs_5_ = bf16[8,128,256]{2,1,0:T(8,128)(2,1)S(1)} collective-permute-done((bf16[8,128,256]{2,1,0:T(8,128)(2,1)S(1)}, bf16[8,128,256]{2,1,0:T(8,128)(2,1)S(1)}, u32[]{:S(2)}, u32[]{:S(2)}) %collective-permute-start.9) | collective-permute-done | bytes 524320 | tf_op jit(solution)/shard_map/ppermute | solution.py:510
  223.1 13.9 %collective-permute-start.12 = (bf16[8,128,256]{2,1,0:T(8,128)(2,1)S(1)}, bf16[8,128,256]{2,1,0:T(8,128)(2,1)S(1)}, u32[]{:S(2)}, u32[]{:S(2)}) collective-permute-start(bf16[8,128,256]{2,1,0:T(8,128)(2,1)S(1)} %bitcast.51), channel_id=1, source_target_pairs={{0,16},{16,0},{32,48},{48,32},{64,80},{80,64},{96,112},{112,96},{1... | collective-permute-start | bytes 1572872 | tf_op jit(solution)/shard_map/ppermute | solution.py:510
  237.0 0.1 collective-permute-start.10
  237.2 0.1 collective-permute-start.13
  237.3 0.5 collective-permute-start.14
  237.8 1.2 collective-permute-start.11
  239.0 6.1 %collective-permute-done.10.refs_6_ = bf16[4,128,256]{2,1,0:T(8,128)(2,1)S(1)} collective-permute-done((bf16[4,128,256]{2,1,0:T(8,128)(2,1)S(1)}, bf16[4,128,256]{2,1,0:T(8,128)(2,1)S(1)}, u32[]{:S(2)}, u32[]{:S(2)}) %collective-permute-start.10) | collective-permute-done | bytes 262176 | tf_op jit(solution)/shard_map/ppermute | solution.py:510
  245.1 0.8 collective-permute-start.15
  245.8 1.0 collective-permute-done.11.refs_7_
  246.8 0.9 collective-permute-start.16
  247.7 1.1 collective-permute-done.16.refs_12_
  248.9 17.9 %lab_step.1 = bf16[128,16,256]{2,1,0:T(8,128)(2,1)} custom-call(s32[1]{0:T(128)} %bitcast.11.row_ref, bf16[129,16,128]{2,1,0:T(8,128)(2,1)S(1)} %copy-done.5, bf16[4,129,16,128]{3,2,1,0:T(8,128)(2,1)} %collective-permute-done.4.other_any, bf16[2,129,16,128]{3,2,1,0:T(8,128)(2,1)} %collective-permute-done.5.refs_0_, ...), custom_call_target="tpu_custom_call" | custom-call | tf_op jit(solution)/shard_map/lab_step/pallas_call | solution.py:662
  266.8 4.0 %all-to-all-start.6 = ((bf16[8,256,256]{2,1,0:T(8,128)(2,1)}), bf16[8,256,256]{2,1,0:T(8,128)(2,1)S(1)}, u32[]{:S(2)}, u32[]{:S(2)}) async-start(bf16[8,256,256]{2,1,0:T(8,128)(2,1)} %bitcast.23), calls=%async_computation.6 | async-start | bytes 2097152 | tf_op jit(solution)/shard_map/all_to_all | solution.py:686
  270.7 0.6 slice_bitcast_fusion.1
  271.4 14.5 %all-to-all-done.6 = bf16[8,256,256]{2,1,0:T(8,128)(2,1)S(1)} async-done(((bf16[8,256,256]{2,1,0:T(8,128)(2,1)}), bf16[8,256,256]{2,1,0:T(8,128)(2,1)S(1)}, u32[]{:S(2)}, u32[]{:S(2)}) %all-to-all-start.6) | async-done | bytes 1048608 | tf_op jit(solution)/shard_map/all_to_all | solution.py:686
  285.9 0.3 fusion
  286.2 1.5 copy.27
  (43 shorter events, 0.2 us)
Async XLA Ops:
  7.2 64.9 %copy-start = (bf16[256,256]{1,0:T(8,128)(2,1)S(1)}, bf16[256,256]{1,0:T(8,128)(2,1)}, u32[]{:S(2)}) copy-start(bf16[256,256]{1,0:T(8,128)(2,1)} %param.19) | copy-start | bytes 393220
  7.2 70.3 %all-gather.2.cloned.1.call-start = ((), (), s32[]{:S(2)}) async-start(), calls=%async_computation.7 | async-start | bytes 7077888 | tf_op jit(solution)/shard_map/all_gather | solution.py:544
  31.1 18.6 %collective-permute-start = (bf16[16,32,256]{2,1,0:T(8,128)(2,1)S(1)}, bf16[16,32,256]{2,1,0:T(8,128)(2,1)S(1)}, u32[]{:S(2)}, u32[]{:S(2)}) collective-permute-start(bf16[16,32,256]{2,1,0:T(8,128)(2,1)S(1)} %slice.37), channel_id=1, source_target_pairs={{0,32},{16,48},{32,0},{48,16},{64,96},{80,112},{96,64},{112,80},{1... | collective-permute-start | bytes 786440 | tf_op jit(solution)/shard_map/ppermute | solution.py:510
  32.5 17.2 %collective-permute-start.1 = (bf16[16,32,256]{2,1,0:T(8,128)(2,1)S(1)}, bf16[16,32,256]{2,1,0:T(8,128)(2,1)S(1)}, u32[]{:S(2)}, u32[]{:S(2)}) collective-permute-start(bf16[16,32,256]{2,1,0:T(8,128)(2,1)S(1)} %slice.37), channel_id=1, source_target_pairs={{0,64},{16,80},{32,96},{48,112},{64,0},{80,16},{96,32},{112,48},{1... | collective-permute-start | bytes 786440 | tf_op jit(solution)/shard_map/ppermute | solution.py:510
  35.1 14.6 %collective-permute-start.2 = (bf16[16,32,256]{2,1,0:T(8,128)(2,1)S(1)}, bf16[16,32,256]{2,1,0:T(8,128)(2,1)S(1)}, u32[]{:S(2)}, u32[]{:S(2)}) collective-permute-start(bf16[16,32,256]{2,1,0:T(8,128)(2,1)S(1)} %slice.37), channel_id=1, source_target_pairs={{0,96},{16,112},{32,64},{48,80},{64,32},{80,48},{96,0},{112,16},{1... | collective-permute-start | bytes 786440 | tf_op jit(solution)/shard_map/ppermute | solution.py:510
  47.1 27.1 %collective-permute-start.4 = (bf16[4,129,16,128]{3,2,1,0:T(8,128)(2,1)}, bf16[4,129,16,128]{3,2,1,0:T(8,128)(2,1)}, u32[]{:S(2)}, u32[]{:S(2)}) collective-permute-start(bf16[4,129,16,128]{3,2,1,0:T(8,128)(2,1)} %get-tuple-element.185), channel_id=1, source_target_pairs={{0,16},{16,0},{32,48},{48,32},{64,80},{80,64},{96,112},{112,96},{1... | collective-permute-start | bytes 6340616 | tf_op jit(solution)/shard_map/ppermute | solution.py:510
  65.1 12.3 %copy-start.1 = (bf16[16,4,32,256]{3,2,1,0:T(8,128)(2,1)}, bf16[16,4,32,256]{3,2,1,0:T(8,128)(2,1)S(1)}, u32[]{:S(2)}) copy-start(bf16[16,4,32,256]{3,2,1,0:T(8,128)(2,1)S(1)} %all_to_all.59.here_any.refs_14_) | copy-start | bytes 3145732
  65.1 9.1 %collective-permute-start.3 = (bf16[16,4,32,256]{3,2,1,0:T(8,128)(2,1)S(1)}, bf16[16,4,32,256]{3,2,1,0:T(8,128)(2,1)S(1)}, u32[]{:S(2)}, u32[]{:S(2)}) collective-permute-start(bf16[16,4,32,256]{3,2,1,0:T(8,128)(2,1)S(1)} %all_to_all.59.here_any.refs_14_), channel_id=1, source_target_pairs={{0,16},{16,0},{32,48},{48,32},{64,80},{80,64},{96,112},{112,96},{1... | collective-permute-start | bytes 3145736 | tf_op jit(solution)/shard_map/ppermute | solution.py:510
  74.2 3.2 %copy-start.3 = (bf16[16,4,32,256]{3,2,1,0:T(8,128)(2,1)}, bf16[16,4,32,256]{3,2,1,0:T(8,128)(2,1)S(1)}, u32[]{:S(2)}) copy-start(bf16[16,4,32,256]{3,2,1,0:T(8,128)(2,1)S(1)} %collective-permute-done.3.there_any.refs_15_) | copy-start | bytes 3145732
  85.3 20.1 %all-to-all-start.4 = ((f32[16,64,256]{2,1,0:T(8,128)}), f32[16,64,256]{2,1,0:T(8,128)S(1)}, u32[]{:S(2)}, u32[]{:S(2)}) async-start(f32[16,64,256]{2,1,0:T(8,128)} %bitcast.60), calls=%async_computation.4 | async-start | bytes 2097152 | tf_op jit(solution)/shard_map/all_to_all | solution.py:573
  90.0 1.7 copy-start.10
  90.0 2.8 copy-start.9
  91.8 2.2 copy-start.8
  92.8 144.3 %collective-permute-start.5 = (bf16[2,129,16,128]{3,2,1,0:T(8,128)(2,1)}, bf16[2,129,16,128]{3,2,1,0:T(8,128)(2,1)}, u32[]{:S(2)}, u32[]{:S(2)}) collective-permute-start(bf16[2,129,16,128]{3,2,1,0:T(8,128)(2,1)} %pad_maximum_fusion), channel_id=1, source_target_pairs={{0,32},{16,48},{32,0},{48,16},{64,96},{80,112},{96,64},{112,80},{1... | collective-permute-start | bytes 3170312 | tf_op jit(solution)/shard_map/ppermute | solution.py:510
  92.8 6.0 %copy-start.2 = (bf16[16,4,32,256]{3,2,1,0:T(8,128)(2,1)S(1)}, bf16[16,4,32,256]{3,2,1,0:T(8,128)(2,1)}, u32[]{:S(2)}) copy-start(bf16[16,4,32,256]{3,2,1,0:T(8,128)(2,1)} %copy-done.1) | copy-start | bytes 3145732
  92.8 6.0 %copy-start.6 = (bf16[16,96,256]{2,1,0:T(8,128)(2,1)S(1)}, bf16[16,96,256]{2,1,0:T(8,128)(2,1)}, u32[]{:S(2)}) copy-start(bf16[16,96,256]{2,1,0:T(8,128)(2,1)} %all_to_all.58) | copy-start | bytes 2359300
  93.9 143.3 %collective-permute-start.6 = (bf16[2,129,16,128]{3,2,1,0:T(8,128)(2,1)}, bf16[2,129,16,128]{3,2,1,0:T(8,128)(2,1)}, u32[]{:S(2)}, u32[]{:S(2)}) collective-permute-start(bf16[2,129,16,128]{3,2,1,0:T(8,128)(2,1)} %pad_maximum_fusion.1), channel_id=1, source_target_pairs={{0,64},{16,80},{32,96},{48,112},{64,0},{80,16},{96,32},{112,48},{1... | collective-permute-start | bytes 3170312 | tf_op jit(solution)/shard_map/ppermute | solution.py:510
  95.0 142.8 %collective-permute-start.7 = (bf16[2,129,16,128]{3,2,1,0:T(8,128)(2,1)}, bf16[2,129,16,128]{3,2,1,0:T(8,128)(2,1)}, u32[]{:S(2)}, u32[]{:S(2)}) collective-permute-start(bf16[2,129,16,128]{3,2,1,0:T(8,128)(2,1)} %pad_maximum_fusion.2), channel_id=1, source_target_pairs={{0,96},{16,112},{32,64},{48,80},{64,32},{80,48},{96,0},{112,16},{1... | collective-permute-start | bytes 3170312 | tf_op jit(solution)/shard_map/ppermute | solution.py:510
  124.2 13.4 %all-to-all-start.1 = ((bf16[16,64,256]{2,1,0:T(8,128)(2,1)}), bf16[16,64,256]{2,1,0:T(8,128)(2,1)S(1)}, u32[]{:S(2)}, u32[]{:S(2)}) async-start(bf16[16,64,256]{2,1,0:T(8,128)(2,1)} %bitcast.47), calls=%async_computation.1 | async-start | bytes 1048576 | tf_op jit(solution)/shard_map/while/body/eval_jaxpr/all_to_all | solution.py:573
  155.8 13.3 %all-to-all-start.1 = ((bf16[16,64,256]{2,1,0:T(8,128)(2,1)}), bf16[16,64,256]{2,1,0:T(8,128)(2,1)S(1)}, u32[]{:S(2)}, u32[]{:S(2)}) async-start(bf16[16,64,256]{2,1,0:T(8,128)(2,1)} %bitcast.47), calls=%async_computation.1 | async-start | bytes 1048576 | tf_op jit(solution)/shard_map/while/body/eval_jaxpr/all_to_all | solution.py:573
  186.9 13.3 %all-to-all-start.1 = ((bf16[16,64,256]{2,1,0:T(8,128)(2,1)}), bf16[16,64,256]{2,1,0:T(8,128)(2,1)S(1)}, u32[]{:S(2)}, u32[]{:S(2)}) async-start(bf16[16,64,256]{2,1,0:T(8,128)(2,1)} %bitcast.47), calls=%async_computation.1 | async-start | bytes 1048576 | tf_op jit(solution)/shard_map/while/body/eval_jaxpr/all_to_all | solution.py:573
  200.4 48.5 %copy-start.4 = (bf16[16,4,32,256]{3,2,1,0:T(8,128)(2,1)S(1)}, bf16[16,4,32,256]{3,2,1,0:T(8,128)(2,1)}, u32[]{:S(2)}) copy-start(bf16[16,4,32,256]{3,2,1,0:T(8,128)(2,1)} %copy-done.3) | copy-start | bytes 3145732
  200.4 48.4 %copy-start.5 = (bf16[129,16,128]{2,1,0:T(8,128)(2,1)S(1)}, bf16[129,16,128]{2,1,0:T(8,128)(2,1)}, u32[]{:S(2)}) copy-start(bf16[129,16,128]{2,1,0:T(8,128)(2,1)} %get-tuple-element.202.same_any) | copy-start | bytes 1585156
  213.6 9.5 %collective-permute-start.9 = (bf16[8,128,256]{2,1,0:T(8,128)(2,1)S(1)}, bf16[8,128,256]{2,1,0:T(8,128)(2,1)S(1)}, u32[]{:S(2)}, u32[]{:S(2)}) collective-permute-start(bf16[8,128,256]{2,1,0:T(8,128)(2,1)S(1)} %bitcast.49), channel_id=1, source_target_pairs={{0,96},{16,112},{32,64},{48,80},{64,32},{80,48},{96,0},{112,16},{1... | collective-permute-start | bytes 1572872 | tf_op jit(solution)/shard_map/ppermute | solution.py:510
  213.6 23.4 %collective-permute-start.8 = (bf16[8,128,256]{2,1,0:T(8,128)(2,1)S(1)}, bf16[8,128,256]{2,1,0:T(8,128)(2,1)S(1)}, u32[]{:S(2)}, u32[]{:S(2)}) collective-permute-start(bf16[8,128,256]{2,1,0:T(8,128)(2,1)S(1)} %bitcast.50), channel_id=1, source_target_pairs={{0,32},{16,48},{32,0},{48,16},{64,96},{80,112},{96,64},{112,80},{1... | collective-permute-start | bytes 1572872 | tf_op jit(solution)/shard_map/ppermute | solution.py:510
  223.1 24.6 %collective-permute-start.12 = (bf16[8,128,256]{2,1,0:T(8,128)(2,1)S(1)}, bf16[8,128,256]{2,1,0:T(8,128)(2,1)S(1)}, u32[]{:S(2)}, u32[]{:S(2)}) collective-permute-start(bf16[8,128,256]{2,1,0:T(8,128)(2,1)S(1)} %bitcast.51), channel_id=1, source_target_pairs={{0,16},{16,0},{32,48},{48,32},{64,80},{80,64},{96,112},{112,96},{1... | collective-permute-start | bytes 1572872 | tf_op jit(solution)/shard_map/ppermute | solution.py:510
  237.0 8.0 %collective-permute-start.10 = (bf16[4,128,256]{2,1,0:T(8,128)(2,1)S(1)}, bf16[4,128,256]{2,1,0:T(8,128)(2,1)S(1)}, u32[]{:S(2)}, u32[]{:S(2)}) collective-permute-start(bf16[4,128,256]{2,1,0:T(8,128)(2,1)S(1)} %slice.38), channel_id=1, source_target_pairs={{0,32},{16,48},{32,0},{48,16},{64,96},{80,112},{96,64},{112,80},{1... | collective-permute-start | bytes 786440 | tf_op jit(solution)/shard_map/ppermute | solution.py:510
  237.2 10.6 %collective-permute-start.13 = (bf16[8,128,256]{2,1,0:T(8,128)(2,1)S(1)}, bf16[8,128,256]{2,1,0:T(8,128)(2,1)S(1)}, u32[]{:S(2)}, u32[]{:S(2)}) collective-permute-start(bf16[8,128,256]{2,1,0:T(8,128)(2,1)S(1)} %collective-permute-done.8.refs_4_), channel_id=1, source_target_pairs={{0,16},{16,0},{32,48},{48,32},{64,80},{80,64},{96,112},{112,96},{1... | collective-permute-start | bytes 1572872 | tf_op jit(solution)/shard_map/ppermute | solution.py:510
  237.3 10.5 %collective-permute-start.14 = (bf16[8,128,256]{2,1,0:T(8,128)(2,1)S(1)}, bf16[8,128,256]{2,1,0:T(8,128)(2,1)S(1)}, u32[]{:S(2)}, u32[]{:S(2)}) collective-permute-start(bf16[8,128,256]{2,1,0:T(8,128)(2,1)S(1)} %collective-permute-done.9.refs_5_), channel_id=1, source_target_pairs={{0,16},{16,0},{32,48},{48,32},{64,80},{80,64},{96,112},{112,96},{1... | collective-permute-start | bytes 1572872 | tf_op jit(solution)/shard_map/ppermute | solution.py:510
  237.8 9.1 %collective-permute-start.11 = (bf16[4,128,256]{2,1,0:T(8,128)(2,1)S(1)}, bf16[4,128,256]{2,1,0:T(8,128)(2,1)S(1)}, u32[]{:S(2)}, u32[]{:S(2)}) collective-permute-start(bf16[4,128,256]{2,1,0:T(8,128)(2,1)S(1)} %slice.39), channel_id=1, source_target_pairs={{0,96},{16,112},{32,64},{48,80},{64,32},{80,48},{96,0},{112,16},{1... | collective-permute-start | bytes 786440 | tf_op jit(solution)/shard_map/ppermute | solution.py:510
  245.1 2.7 collective-permute-start.15
  246.8 2.0 collective-permute-start.16
  266.7 19.1 %copy-start.7 = (bf16[16,128,256]{2,1,0:T(8,128)(2,1)S(1)}, bf16[16,128,256]{2,1,0:T(8,128)(2,1)}, u32[]{:S(2)}) copy-start(bf16[16,128,256]{2,1,0:T(8,128)(2,1)} %pad_maximum_fusion.4) | copy-start | bytes 3145732
  266.8 19.1 %all-to-all-start.6 = ((bf16[8,256,256]{2,1,0:T(8,128)(2,1)}), bf16[8,256,256]{2,1,0:T(8,128)(2,1)S(1)}, u32[]{:S(2)}, u32[]{:S(2)}) async-start(bf16[8,256,256]{2,1,0:T(8,128)(2,1)} %bitcast.23), calls=%async_computation.6 | async-start | bytes 2097152 | tf_op jit(solution)/shard_map/all_to_all | solution.py:686
Sparse Core Ops, SparseCore 0:
  30.3 47.1 all-gather.1
